TPU v7x, 256 devices: a whole 4x4x8 slice. The times are simulated.
256 devices in a mesh: section: 32 (over y, z), dp: 8 (over x, core).
Axes of the slice: x: 4, y: 4, z: 8, core: 2. Of those that a mesh axis runs over, the one named last changes fastest.
Arguments:
- stash: bfloat16 [2, 32, 8, 128, 5120], P(None, 'section', None, 'dp'), may hold values from -6 to 6
- cotangent: bfloat16 [8, 128, 5120], P(None, 'dp', 'section'), may hold values from -6 to 6
- a_param: float32 [2, 32, 5120, 128], P(None, 'section', 'dp'), may hold values from -0.078125 to 0.078125
- a_moment: float32 [2, 32, 5120, 128], P(None, 'section', 'dp'), may hold values from -3 to 3
- a_second: float32 [2, 32, 5120, 128], P(None, 'section', 'dp'), may hold values from 0.01 to 1
- b_param: float32 [2, 32, 128, 5120], P(None, 'section', None, 'dp'), may hold values from -0.109375 to 0.109375
- b_moment: float32 [2, 32, 128, 5120], P(None, 'section', None, 'dp'), may hold values from -3 to 3
- b_second: float32 [2, 32, 128, 5120], P(None, 'section', None, 'dp'), may hold values from 0.01 to 1
Outputs:
- new_a_param: float32 [2, 32, 5120, 128], P(None, 'section', 'dp')
- new_a_moment: float32 [2, 32, 5120, 128], P(None, 'section', 'dp')
- new_a_second: float32 [2, 32, 5120, 128], P(None, 'section', 'dp')
- new_b_param: float32 [2, 32, 128, 5120], P(None, 'section', None, 'dp')
- new_b_moment: float32 [2, 32, 128, 5120], P(None, 'section', None, 'dp')
- new_b_second: float32 [2, 32, 128, 5120], P(None, 'section', None, 'dp')
- grad_norm: float32 [], replicated
All inputs are finite; a program needn't handle non-finite values.
Results may differ from a plain program's by a relative error of at most 0.013.
Values may be sent and summed in bfloat16 or wider, within the bound.
A program may use at most 128 MiB of HBM per device.

v0:
```python
import math

import jax
import jax.numpy as jnp
from jax import lax
from jax.sharding import PartitionSpec as P

beta_one = 0.9
beta_two = 0.95
learning_rate = 0.01
adam_epsilon = 1e-08
norm_epsilon = 1e-06


def from_behind(value, axis, steps):
    count = lax.axis_size(axis)
    initial, last = (max(0, -steps), min(count, count - steps))
    return lax.ppermute(value, axis, [(source, source + steps) for source in range(initial, last)])


def normed_parts(inputs):
    values = inputs.astype(jnp.float32)
    inv_rms = lax.rsqrt(jnp.mean(values * values, axis=-1, keepdims=True) + norm_epsilon)
    normed_f = values * inv_rms
    return (inv_rms, normed_f, normed_f.astype(jnp.bfloat16))


def block_backward(inputs, incoming, a_weight, b_weight):
    inv_rms, normed_f, normed = normed_parts(inputs)
    preact = jnp.dot(normed, a_weight, preferred_element_type=jnp.float32)
    gate_sig = jax.nn.sigmoid(preact)
    hidden = (preact * gate_sig).astype(jnp.bfloat16)
    grad_hidden = jnp.dot(incoming, b_weight.T, preferred_element_type=jnp.float32)
    grad_pre = (grad_hidden * gate_sig * (1.0 + preact * (1.0 - gate_sig))).astype(jnp.bfloat16)
    grad_normed = jnp.dot(grad_pre, a_weight.T, preferred_element_type=jnp.float32)
    inner_mean = jnp.mean(grad_normed * normed_f, axis=-1, keepdims=True)
    outgoing = (
        incoming.astype(jnp.float32) + inv_rms * (grad_normed - normed_f * inner_mean)
    ).astype(jnp.bfloat16)
    return (outgoing, normed, hidden, grad_pre)


def adam_update(param, moment, second, grad, clip_factor):
    scaled = clip_factor * grad
    moment_new = beta_one * moment + (1.0 - beta_one) * scaled
    second_new = beta_two * second + (1.0 - beta_two) * scaled * scaled
    param_new = param - learning_rate * moment_new / (jnp.sqrt(second_new) + adam_epsilon)
    return (param_new, moment_new, second_new)


def place_row(store, which, index_now, valid, value):
    part = store[which]
    previous = lax.dynamic_index_in_dim(part, index_now, 0, keepdims=False)
    kept = jnp.where(valid, value, previous)
    return store.at[which].set(lax.dynamic_update_index_in_dim(part, kept, index_now, 0))


def shards(stash, cotangent, a_param, a_moment, a_second, b_param, b_moment, b_second):
    sections = lax.axis_size("section")
    position = lax.axis_index("section")
    a_full, b_full = (
        lax.all_gather(a_param.astype(jnp.bfloat16), "dp", axis=2, tiled=True),
        lax.all_gather(b_param.astype(jnp.bfloat16), "dp", axis=3, tiled=True),
    )
    a_weights = a_full[:, 0]
    b_weights = b_full[:, 0]
    first_deltas = lax.all_gather(cotangent, "section", axis=2, tiled=True)
    micro_count, tok_rows, model_width = first_deltas.shape
    rank_size = a_param.shape[3]
    local_inputs = stash[:, 0]
    empty_rows = jnp.zeros((tok_rows, model_width), jnp.bfloat16)
    empty_small = jnp.zeros((tok_rows, rank_size), jnp.bfloat16)

    def busy(inputs, incoming, a_weight, b_weight):
        outgoing, normed, hidden, grad_pre = block_backward(inputs, incoming, a_weight, b_weight)
        return (outgoing, hidden, grad_pre)

    def resting(inputs, incoming, a_weight, b_weight):
        return (empty_rows, empty_small, empty_small)

    def run_block(which, offset, incoming, stores):
        valid = (offset >= 0) & (offset < micro_count)
        clamped = jnp.clip(offset, 0, micro_count - 1)
        inputs = lax.dynamic_index_in_dim(local_inputs[which], clamped, 0, keepdims=False)
        outgoing, hidden, grad_pre = lax.cond(
            valid, busy, resting, inputs, incoming, a_weights[which], b_weights[which]
        )
        store_delta, store_hidden, store_pre = stores
        store_delta = place_row(store_delta, which, clamped, valid, incoming)
        store_hidden = place_row(store_hidden, which, clamped, valid, hidden)
        store_pre = place_row(store_pre, which, clamped, valid, grad_pre)
        return (outgoing, (store_delta, store_hidden, store_pre))

    def make_tick(upper_on, lower_on):

        def tick_step(moment, carry):
            up_in, low_in, stores = carry
            up_out = empty_rows
            low_out = empty_rows
            if upper_on:
                up_offset = moment - position
                start_delta = lax.dynamic_index_in_dim(
                    first_deltas, jnp.clip(up_offset, 0, micro_count - 1), 0, keepdims=False
                )
                up_delta = jnp.where(position == 0, start_delta, up_in)
                up_out, stores = run_block(1, up_offset, up_delta, stores)
            if lower_on:
                low_offset = moment - (2 * sections - 1 - position)
                low_out, stores = run_block(0, low_offset, low_in, stores)
            if upper_on:
                up_next = from_behind(up_out, "section", 1)
            else:
                up_next = up_in
            if lower_on:
                low_recv = from_behind(low_out, "section", -1)
            else:
                low_recv = empty_rows
            if upper_on:
                low_next = jnp.where(position == sections - 1, up_out, low_recv)
            else:
                low_next = low_recv
            return (up_next, low_next, stores)

        return tick_step

    stores_init = (
        jnp.zeros((2, micro_count, tok_rows, model_width), jnp.bfloat16),
        jnp.zeros((2, micro_count, tok_rows, rank_size), jnp.bfloat16),
        jnp.zeros((2, micro_count, tok_rows, rank_size), jnp.bfloat16),
    )
    carry = (empty_rows, empty_rows, stores_init)
    carry = lax.fori_loop(0, sections, make_tick(True, False), carry)
    carry = lax.fori_loop(sections, sections + micro_count - 1, make_tick(True, True), carry)
    carry = lax.fori_loop(
        sections + micro_count - 1, 2 * sections + micro_count - 1, make_tick(False, True), carry
    )
    store_delta, store_hidden, store_pre = carry[2]
    flat_rows = micro_count * tok_rows
    normed = normed_parts(local_inputs.reshape(2, flat_rows, model_width))[2]
    deltas = store_delta.reshape(2, flat_rows, model_width)
    hiddens = store_hidden.reshape(2, flat_rows, rank_size)
    pres = store_pre.reshape(2, flat_rows, rank_size)
    partial_a = jnp.einsum("htd,htr->hdr", normed, pres, preferred_element_type=jnp.float32)
    partial_b = jnp.einsum("htr,htd->hrd", hiddens, deltas, preferred_element_type=jnp.float32)
    grad_a, grad_b = (
        lax.psum_scatter(
            partial_a.astype(jnp.bfloat16), "dp", scatter_dimension=1, tiled=True
        ).astype(jnp.float32),
        lax.psum_scatter(
            partial_b.astype(jnp.bfloat16), "dp", scatter_dimension=2, tiled=True
        ).astype(jnp.float32),
    )
    local_squares = jnp.sum(grad_a * grad_a) + jnp.sum(grad_b * grad_b)
    square_total = lax.psum(local_squares, ("section", "dp"))
    grad_norm = jnp.sqrt(square_total)
    entries = 4 * sections * model_width * rank_size
    clip_factor = jnp.minimum(1.0, 0.5 * math.sqrt(entries) / grad_norm)
    a_new, a_moment_new, a_second_new = adam_update(
        a_param, a_moment, a_second, grad_a[:, None], clip_factor
    )
    b_new, b_moment_new, b_second_new = adam_update(
        b_param, b_moment, b_second, grad_b[:, None], clip_factor
    )
    return (a_new, a_moment_new, a_second_new, b_new, b_moment_new, b_second_new, grad_norm)


def solution(mesh):
    return jax.shard_map(
        shards,
        mesh=mesh,
        in_specs=(
            P(None, "section", None, "dp", None),
            P(None, "dp", "section"),
            P(None, "section", "dp", None),
            P(None, "section", "dp", None),
            P(None, "section", "dp", None),
            P(None, "section", None, "dp"),
            P(None, "section", None, "dp"),
            P(None, "section", None, "dp"),
        ),
        out_specs=(
            P(None, "section", "dp", None),
            P(None, "section", "dp", None),
            P(None, "section", "dp", None),
            P(None, "section", None, "dp"),
            P(None, "section", None, "dp"),
            P(None, "section", None, "dp"),
            P(),
        ),
        check_vma=False,
    )
```

profile of v0, /device:TPU:1, one launch (start us, length us, event | category | flops | bytes accessed | tf_op | source)
XLA Modules:
  0.0 1462.6 jit_solution(2765933834810271333)
XLA Ops:
  11.9 111.8 %all-gather.4.cloned.1.call-done = bf16[8,16,5120]{1,0,2:T(8,128)(2,1)} async-done(((bf16[8,16,160]{1,0,2:T(8,128)(2,1)}), bf16[8,16,5120]{1,0,2:T(8,128)(2,1)}) %all-gather.4.cloned.1.call-update) | async-done | bytes 1310736 | tf_op jit(solution)/shard_map/all_gather | solution.py:67
  123.7 9.9 copy.36
  133.6 19.1 %all-gather.8.cloned.1.call-done = bf16[2,1,5120,128]{3,2,0,1:T(8,128)(2,1)} async-done(((bf16[2,1,640,128]{3,2,0,1:T(8,128)(2,1)}), bf16[2,1,5120,128]{3,2,0,1:T(8,128)(2,1)}) %all-gather.8.cloned.1.call-update) | async-done | bytes 2621456 | tf_op jit(solution)/shard_map/all_gather | solution.py:62
  152.7 31.9 %all-gather.6.cloned.1.call-done = bf16[2,1,128,5120]{3,2,0,1:T(8,128)(2,1)} async-done(((bf16[2,1,128,640]{3,2,0,1:T(8,128)(2,1)}), bf16[2,1,128,5120]{3,2,0,1:T(8,128)(2,1)}) %all-gather.6.cloned.1.call-update) | async-done | bytes 2621456 | tf_op jit(solution)/shard_map/all_gather | solution.py:63
  187.4 473.6 %while.79 = (s32[]{:T(128)}, bf16[16,5120]{1,0:T(8,128)(2,1)S(1)}, bf16[16,5120]{1,0:T(8,128)(2,1)}, bf16[2,8,16,5120]{3,2,1,0:T(8,128)(2,1)}, bf16[2,8,16,128]{...) while((s32[]{:T(128)}, bf16[16,5120]{1,0:T(8,128)(2,1)S(1)}, ...), condition=%wide.region_6.7_spmd, body=%wide.region_1.6_spmd.sunk | while | flops 64667672 | bytes 37035420 | solution.py:132
  322.2 7.2 collective-permute-start
  351.4 7.2 collective-permute-start
  380.6 7.2 collective-permute-start
  409.8 7.3 collective-permute-start
  524.3 8.4 collective-permute-start
  660.9 132.1 %while.80 = (s32[]{:T(128)}, bf16[16,5120]{1,0:T(8,128)(2,1)S(1)}, bf16[16,5120]{1,0:T(8,128)(2,1)}, bf16[2,8,16,5120]{3,2,1,0:T(8,128)(2,1)}, bf16[2,8,16,128]{...) while((s32[]{:T(128)}, bf16[16,5120]{1,0:T(8,128)(2,1)S(1)}, ...), condition=%wide.region_16.17_spmd, body=%wide.region_7.16_spmd.sunk | while | flops 129171496 | bytes 79769872 | solution.py:133
  704.6 6.0 collective-permute-start.1
  723.6 5.9 collective-permute-start.1
  761.2 6.8 collective-permute-start.1
  780.9 6.0 collective-permute-start.1
  793.0 431.2 %while.81 = (s32[]{:T(128)}, bf16[16,5120]{1,0:T(8,128)(2,1)}, bf16[2,8,16,5120]{3,2,1,0:T(8,128)(2,1)}, bf16[2,8,16,128]{3,2,1,0:T(8,128)(2,1)S(1)}, bf16[2,8,1...) while((s32[]{:T(128)}, bf16[16,5120]{1,0:T(8,128)(2,1)}, ...), condition=%wide.region_22.23_spmd, body=%wide.region_17.22_spmd.sunk | while | flops 64503832 | bytes 38017484 | solution.py:134
  865.6 6.3 collective-permute-done.3
  975.4 6.3 collective-permute-done.3
  1025.1 86.3 %collective-permute-done.3 = bf16[16,5120]{1,0:T(8,128)(2,1)S(1)} collective-permute-done((bf16[16,5120]{1,0:T(8,128)(2,1)S(1)}, bf16[16,5120]{1,0:T(8,128)(2,1)S(1)}, u32[]{:S(2)}, u32[]{:S(2)}) %collective-permute-start.3) | collective-permute-done | bytes 163872 | tf_op jit(solution)/shard_map/while/body/eval_jaxpr/ppermute | solution.py:18
  1149.7 9.1 collective-permute-done.3
  1228.4 7.4 copy.51
  1248.4 81.7 %reduce-scatter.7.cloned.1.call-done = bf16[640,256]{1,0:T(8,128)(2,1)} async-done(((bf16[5120,256]{1,0:T(8,128)(2,1)}), bf16[640,256]{1,0:T(8,128)(2,1)}) %reduce-scatter.7.cloned.1.call-update) | async-done | bytes 327696
  1332.9 35.7 %reduce-scatter.5.cloned.1.call-done = bf16[2,640,128]{2,1,0:T(8,128)(2,1)} async-done(((bf16[2,5120,128]{2,1,0:T(8,128)(2,1)}), bf16[2,640,128]{2,1,0:T(8,128)(2,1)}) %reduce-scatter.5.cloned.1.call-update) | async-done | bytes 327696 | tf_op jit(solution)/shard_map/reduce_scatter | solution.py:146
  1371.7 78.7 %psum.7 = f32[]{:T(128)} all-reduce(f32[]{:T(128)S(6)} %add.291), channel_id=1, replica_groups=mesh['section'=32,'dp'=8] {'section','dp'}, use_global_device_ids=true, to_apply=%region_27.28 | all-reduce | flops 1 | bytes 8 | tf_op jit(solution)/shard_map/psum | solution.py:154
  (1671 shorter events, 1007.7 us)
Async XLA Ops:
  7.2 116.6 %all-gather.4.cloned.1.call-start = ((), (), s32[]{:S(2)}) async-start(), calls=%async_computation.2 | async-start | bytes 10813440 | tf_op jit(solution)/shard_map/all_gather | solution.py:67
  9.1 143.6 %all-gather.8.cloned.1.call-start = ((), (), s32[]{:S(2)}) async-start(), calls=%async_computation.4 | async-start | bytes 2949120 | tf_op jit(solution)/shard_map/all_gather | solution.py:62
  11.0 173.6 %all-gather.6.cloned.1.call-start = ((), (), s32[]{:S(2)}) async-start(), calls=%async_computation.3 | async-start | bytes 2949120 | tf_op jit(solution)/shard_map/all_gather | solution.py:63
  11.8 1318.3 %reduce-scatter.7.cloned.1.call-start = ((), (), s32[]{:S(2)}) async-start(), calls=%async_computation.6 | async-start | bytes 2949120
  380.6 10.5 collective-permute-start
  409.8 10.5 collective-permute-start
  524.3 11.7 collective-permute-start
  662.3 16.4 %collective-permute-start.2 = (bf16[16,5120]{1,0:T(8,128)(2,1)}, bf16[16,5120]{1,0:T(8,128)(2,1)S(1)}, u32[]{:S(2)}, u32[]{:S(2)}) collective-permute-start(bf16[16,5120]{1,0:T(8,128)(2,1)} %get-tuple-element.1592), channel_id=1, source_target_pairs={{8,0},{16,8},{24,16},{32,24},{40,32},{48,40},{56,48},{64,56},{72,6... | collective-permute-start | bytes 491528 | tf_op jit(solution)/shard_map/while/body/eval_jaxpr/ppermute | solution.py:18
  667.8 11.5 collective-permute-start.1
  680.7 16.4 %collective-permute-start.2 = (bf16[16,5120]{1,0:T(8,128)(2,1)}, bf16[16,5120]{1,0:T(8,128)(2,1)S(1)}, u32[]{:S(2)}, u32[]{:S(2)}) collective-permute-start(bf16[16,5120]{1,0:T(8,128)(2,1)} %get-tuple-element.1592), channel_id=1, source_target_pairs={{8,0},{16,8},{24,16},{32,24},{40,32},{48,40},{56,48},{64,56},{72,6... | collective-permute-start | bytes 491528 | tf_op jit(solution)/shard_map/while/body/eval_jaxpr/ppermute | solution.py:18
  686.2 11.5 collective-permute-start.1
  699.1 16.9 %collective-permute-start.2 = (bf16[16,5120]{1,0:T(8,128)(2,1)}, bf16[16,5120]{1,0:T(8,128)(2,1)S(1)}, u32[]{:S(2)}, u32[]{:S(2)}) collective-permute-start(bf16[16,5120]{1,0:T(8,128)(2,1)} %get-tuple-element.1592), channel_id=1, source_target_pairs={{8,0},{16,8},{24,16},{32,24},{40,32},{48,40},{56,48},{64,56},{72,6... | collective-permute-start | bytes 491528 | tf_op jit(solution)/shard_map/while/body/eval_jaxpr/ppermute | solution.py:18
  704.6 12.1 collective-permute-start.1
  718.0 16.9 %collective-permute-start.2 = (bf16[16,5120]{1,0:T(8,128)(2,1)}, bf16[16,5120]{1,0:T(8,128)(2,1)S(1)}, u32[]{:S(2)}, u32[]{:S(2)}) collective-permute-start(bf16[16,5120]{1,0:T(8,128)(2,1)} %get-tuple-element.1592), channel_id=1, source_target_pairs={{8,0},{16,8},{24,16},{32,24},{40,32},{48,40},{56,48},{64,56},{72,6... | collective-permute-start | bytes 491528 | tf_op jit(solution)/shard_map/while/body/eval_jaxpr/ppermute | solution.py:18
  723.6 12.0 collective-permute-start.1
  736.8 16.8 %collective-permute-start.2 = (bf16[16,5120]{1,0:T(8,128)(2,1)}, bf16[16,5120]{1,0:T(8,128)(2,1)S(1)}, u32[]{:S(2)}, u32[]{:S(2)}) collective-permute-start(bf16[16,5120]{1,0:T(8,128)(2,1)} %get-tuple-element.1592), channel_id=1, source_target_pairs={{8,0},{16,8},{24,16},{32,24},{40,32},{48,40},{56,48},{64,56},{72,6... | collective-permute-start | bytes 491528 | tf_op jit(solution)/shard_map/while/body/eval_jaxpr/ppermute | solution.py:18
  742.4 11.9 collective-permute-start.1
  755.6 17.8 %collective-permute-start.2 = (bf16[16,5120]{1,0:T(8,128)(2,1)}, bf16[16,5120]{1,0:T(8,128)(2,1)S(1)}, u32[]{:S(2)}, u32[]{:S(2)}) collective-permute-start(bf16[16,5120]{1,0:T(8,128)(2,1)} %get-tuple-element.1592), channel_id=1, source_target_pairs={{8,0},{16,8},{24,16},{32,24},{40,32},{48,40},{56,48},{64,56},{72,6... | collective-permute-start | bytes 491528 | tf_op jit(solution)/shard_map/while/body/eval_jaxpr/ppermute | solution.py:18
  761.2 12.9 collective-permute-start.1
  775.4 17.0 %collective-permute-start.2 = (bf16[16,5120]{1,0:T(8,128)(2,1)}, bf16[16,5120]{1,0:T(8,128)(2,1)S(1)}, u32[]{:S(2)}, u32[]{:S(2)}) collective-permute-start(bf16[16,5120]{1,0:T(8,128)(2,1)} %get-tuple-element.1592), channel_id=1, source_target_pairs={{8,0},{16,8},{24,16},{32,24},{40,32},{48,40},{56,48},{64,56},{72,6... | collective-permute-start | bytes 491528 | tf_op jit(solution)/shard_map/while/body/eval_jaxpr/ppermute | solution.py:18
  780.9 12.1 collective-permute-start.1
  1021.0 90.4 %collective-permute-start.3 = (bf16[16,5120]{1,0:T(8,128)(2,1)S(1)}, bf16[16,5120]{1,0:T(8,128)(2,1)S(1)}, u32[]{:S(2)}, u32[]{:S(2)}) collective-permute-start(bf16[16,5120]{1,0:T(8,128)(2,1)S(1)} %get-tuple-element.1609), channel_id=1, source_target_pairs={{8,0},{16,8},{24,16},{32,24},{40,32},{48,40},{56,48},{64,56},{72,6... | collective-permute-start | bytes 491528 | tf_op jit(solution)/shard_map/while/body/eval_jaxpr/ppermute | solution.py:18
  1144.9 13.9 collective-permute-start.3
  1239.5 129.2 %reduce-scatter.5.cloned.1.call-start = ((), (), s32[]{:S(2)}) async-start(), calls=%async_computation.5 | async-start | bytes 2949120 | tf_op jit(solution)/shard_map/reduce_scatter | solution.py:146
  (161 other events, 1282.6 us)
Sparse Core Ops, SparseCore 0:
  11.2 112.5 all-gather.3
  126.1 26.4 all-gather.7
  155.1 29.4 all-gather.5
  1239.6 90.5 reduce-scatter.6
  1332.6 36.0 reduce-scatter.4
where the time goes:
time: 1470 us; the launch traced here: 1460 us
  waiting for transfers between devices  501 us (34%)
  local copies, waits for them, and re-layouts  427 us (29%)
  starting transfers between devices  241 us (16%)
  other arithmetic  116 us (8%)
  blocking collectives  78.7 us (5%)
  matrix products  74.9 us (5%)
  between operations  17.1 us (1%)
    ppermute x78, starting transfers between devices, from_behind(): lax.ppermute(value, axis, [(source, source + steps) for source in range(i...  240 us
    ppermute x78, waiting for transfers between devices, from_behind(): lax.ppermute(value, axis, [(source, source + steps) for source in range(i...  221 us
    slice x234, local copies, waits for them, and re-layouts, place_row(): part = store[which]  147 us
    scatter x163, local copies, waits for them, and re-layouts, place_row(): store.at[which]  144 us
    all_gather x1, waiting for transfers between devices, shards(): first_deltas = lax.all_gather(cotangent, 'section', axis=2, tiled=True)  112 us
    unnamed x6, waiting for transfers between devices  81.8 us
    psum x1, blocking collectives, shards(): square_total = lax.psum(local_squares, ('section', 'dp'))  78.7 us
    dynamic_update_slice x234, other arithmetic, place_row(): lax.dynamic_update_index_in_dim(part, kept, index_now, 0)  74.7 us
  transfers between devices with their start and end apart: 83, of which 38 were waited for; matrix products, arithmetic and copies ran while one was open for 20% of the time, Pallas kernels for 0%

commit v1 on v0

v1 whole, which is shorter than its diff:
```python
import functools
import math

import jax
import jax.numpy as jnp
from jax import lax
from jax.experimental import pallas as pl
from jax.experimental.pallas import tpu as pltpu
from jax.sharding import PartitionSpec as P

beta_one = 0.9
beta_two = 0.95
learning_rate = 0.01
adam_epsilon = 1e-08
norm_epsilon = 1e-06

MESH = pl.DeviceIdType.MESH
F32 = jnp.float32
BF16 = jnp.bfloat16

N_SECTION = 32
N_Z = 8
N_X = 4
N_DP = 8
D = 5120
RANK = 128
MICRO = 8
TILE = 16
SHARD = D // N_DP
FOLD = 4
ROWS = TILE // FOLD
CHUNKS = MICRO * FOLD
WIDE = D // FOLD
PER_PART = WIDE // SHARD
LATE = 16
LAG = 5

NT = (((1,), (1,)), ((), ()))
TN = (((0,), (0,)), ((), ()))


def row_group():
    return lax.broadcasted_iota(jnp.int32, (TILE, RANK), 0) // ROWS


def spread(value):
    step = TILE // 2
    while step >= ROWS:
        value = value + pltpu.roll(value, step, 0)
        step //= 2
    return value


def diagonal(value, group):
    return jnp.concatenate([jnp.where(group == q, value, 0.0) for q in range(FOLD)], axis=1)


def chain_kernel(
    stash, cot, a_param, b_param,
    grad_a, grad_b, total,
    w_b, w_a, x_fold, d_in, d_out, gate, slope, p_diag, h_diag, window,
    keep, pair_out, pair_in, ring_out, ring_in, norm_out, norm_in, lane_out, lane_in, tot_in,
    gat_s, gat_r, ch_s, ch_r, cot_s, cot_r, pair_s, pair_r, ring_s, ring_r, nrm_s, nrm_r, lan_s, lan_r, tot_s, tot_r,
):
    s = lax.axis_index("section")
    d = lax.axis_index("dp")
    x = d // 2
    c = d % 2
    right = lax.rem(x + 1, N_X)
    left = lax.rem(x + N_X - 1, N_X)
    far = lax.rem(x + 2, N_X)
    sib = (s, 2 * x + 1 - c)
    dev_right = (s, 2 * right + c)
    dev_left = (s, 2 * left + c)
    first = s == 0
    last = s == N_SECTION - 1
    down = (jnp.minimum(s + 1, N_SECTION - 1), d)
    up = (jnp.maximum(s - 1, 0), d)
    home = (0, d)
    group = row_group()

    def copy(src, dst, ssem, rsem, dev):
        return pltpu.make_async_remote_copy(
            src_ref=src, dst_ref=dst, send_sem=ssem, recv_sem=rsem, device_id=dev, device_id_type=MESH
        )

    bar = pltpu.get_barrier_semaphore()

    def hello(dev):
        pl.semaphore_signal(bar, inc=1, device_id=dev, device_id_type=MESH)

    hello(sib)
    hello(dev_right)
    hello(dev_left)

    @pl.when(s > 0)
    def _():
        hello(up)
        hello(home)

    @pl.when(s < N_SECTION - 1)
    def _():
        hello(down)

    @pl.when(first)
    def _():
        def lanes(i, carry):
            hello((i, d))
            return carry

        lax.fori_loop(1, N_SECTION, lanes, 0)

        def peers(i, carry):
            hello((0, lax.rem(d + i, N_DP)))
            return carry

        lax.fori_loop(1, N_DP, peers, 0)

    def b_slice(u, e):
        row = pl.multiple_of((e % PER_PART) * SHARD, SHARD)
        col = pl.multiple_of((e // PER_PART) * RANK, RANK)
        return w_b.at[u, pl.ds(row, SHARD), pl.ds(col, RANK)]

    def a_slice(u, e):
        row = pl.multiple_of((e // PER_PART) * RANK, RANK)
        col = pl.multiple_of((e % PER_PART) * SHARD, SHARD)
        return w_a.at[u, pl.ds(row, RANK), pl.ds(col, SHARD)]

    def own_weights(u):
        b_slice(u, d)[...] = b_param[u].T.astype(BF16)
        a_slice(u, d)[...] = a_param[u].T.astype(BF16)

    def refold(get, u, dst, m):
        for at in range(0, WIDE, RANK):
            parts = [get(q, at) for q in range(FOLD)]
            outs = [None] * FOLD
            for q in range(FOLD):
                for j in range(FOLD):
                    turn = (ROWS * (q - j)) % TILE
                    moved = parts[q] if turn == 0 else pltpu.roll(parts[q], turn, 0)
                    outs[j] = moved if q == 0 else jnp.where(group == q, moved, outs[j])
            for j in range(FOLD):
                dst[u, m * FOLD + j, :, at : at + RANK] = outs[j].astype(BF16)

    def fold_stash(u):
        def micro(m, carry):
            refold(lambda q, at: stash[u, m, :, q * WIDE + at : q * WIDE + at + RANK].astype(F32), u, x_fold, m)
            return carry

        lax.fori_loop(0, MICRO, micro, 0)

    own_weights(1)
    own_weights(0)
    fold_stash(1)

    pl.semaphore_wait(
        bar,
        3 + (s > 0).astype(jnp.int32) + (s < N_SECTION - 1).astype(jnp.int32) + jnp.where(first, N_SECTION + N_DP - 2, 1),
    )

    @pl.when(s > 0)
    def _():
        copy(cot, window.at[s], cot_s, cot_r.at[s], home).start()

    def gather_copy(u, slot, xs, cs, kind, dev):
        e = 2 * xs + cs
        ref = b_slice(u, e) if kind == 0 else a_slice(u, e)
        return copy(ref, ref, gat_s.at[u, slot], gat_r.at[u, slot], dev)

    def gather_sends(u):
        return [
            gather_copy(u, 0, x, c, 0, dev_right),
            gather_copy(u, 1, x, c, 1, dev_right),
            gather_copy(u, 2, x, c, 0, dev_left),
            gather_copy(u, 3, x, c, 1, dev_left),
            gather_copy(u, 4, left, c, 0, dev_right),
            gather_copy(u, 5, right, c, 1, dev_left),
        ] + [
            gather_copy(u, 6 + 2 * i + kind, xs, c, kind, sib)
            for i, xs in enumerate((x, left, right, far))
            for kind in (0, 1)
        ]

    def gather_recvs(u):
        return [
            gather_copy(u, 0, left, c, 0, dev_left),
            gather_copy(u, 1, left, c, 1, dev_left),
            gather_copy(u, 2, right, c, 0, dev_right),
            gather_copy(u, 3, right, c, 1, dev_right),
            gather_copy(u, 4, far, c, 0, dev_left),
            gather_copy(u, 5, far, c, 1, dev_right),
        ] + [
            gather_copy(u, 6 + 2 * i + kind, xs, 1 - c, kind, sib)
            for i, xs in enumerate((x, left, right, far))
            for kind in (0, 1)
        ]

    def gather(u):
        out, arr = gather_sends(u), gather_recvs(u)
        out[0].start()
        out[3].start()
        out[1].start()
        out[2].start()
        out[6].start()
        out[7].start()
        arr[0].wait_recv()
        out[4].start()
        out[8].start()
        arr[3].wait_recv()
        out[5].start()
        out[11].start()
        arr[1].wait_recv()
        out[9].start()
        arr[2].wait_recv()
        out[10].start()
        arr[4].wait_recv()
        out[12].start()
        arr[5].wait_recv()
        out[13].start()
        for i in range(6, 14):
            arr[i].wait_recv()

    def gates(u):
        flat = MICRO * TILE
        pre = jnp.zeros((flat, RANK), F32)
        squares = jnp.zeros((flat, 1), F32)
        for e in range(N_DP):
            part = stash[u, :, :, e * SHARD : (e + 1) * SHARD].reshape(flat, SHARD)
            wide = part.astype(F32)
            squares = squares + jnp.sum(wide * wide, axis=1, keepdims=True)
            q, off = e // PER_PART, (e % PER_PART) * SHARD
            pre = pre + lax.dot_general(
                part, w_a[u, q * RANK : (q + 1) * RANK, off : off + SHARD], NT, preferred_element_type=F32
            )
        inv = lax.rsqrt(squares * (1.0 / D) + norm_epsilon)
        pre = pre * inv
        sig = 1.0 / (1.0 + jnp.exp(-pre))
        hidden = pre * sig
        turn = sig * (1.0 + pre * (1.0 - sig)) * inv
        lean = pre * inv * (1.0 / D)
        for m in range(MICRO):
            for j in range(FOLD):
                here = m * FOLD + j
                rows = slice(m * TILE, (m + 1) * TILE)
                gate[u, here] = spread(jnp.where(group == j, turn[rows], 0.0))
                slope[u, here] = spread(jnp.where(group == j, lean[rows], 0.0))
                h_diag[u, here] = diagonal(spread(jnp.where(group == j, hidden[rows], 0.0)), group).astype(BF16)

    def prepare(u):
        gather(u)
        gates(u)

    def chain_copy(u, k, dev):
        return copy(d_out.at[u, k], d_in.at[u, k], ch_s.at[u, k], ch_r.at[u, k], dev)

    def block(u, k):
        incoming = d_in[u, k]
        wide = jnp.dot(incoming, w_b[u], preferred_element_type=F32)
        picked = jnp.where(group == 0, wide[:, :RANK], 0.0)
        for q in range(1, FOLD):
            picked = jnp.where(group == q, wide[:, q * RANK : (q + 1) * RANK], picked)
        grad_hidden = spread(picked)
        grad_pre = (grad_hidden * gate[u, k]).astype(BF16).astype(F32)
        shift = jnp.sum(grad_pre * slope[u, k], axis=1, keepdims=True)
        diag = diagonal(grad_pre, group).astype(BF16)
        p_diag[u, k] = diag
        back = jnp.dot(diag, w_a[u], preferred_element_type=F32)
        return (incoming.astype(F32) + back - x_fold[u, k].astype(F32) * shift).astype(BF16)

    def upper(k):
        @pl.when(s > 0)
        def _():
            chain_copy(1, k, up).wait_recv()

        out = block(1, k)

        @pl.when(last)
        def _():
            d_in[0, k] = out

        @pl.when(s < N_SECTION - 1)
        def _():
            d_out[1, k] = out
            chain_copy(1, k, down).start()

    def lower(k):
        @pl.when(s < N_SECTION - 1)
        def _():
            chain_copy(0, k, down).wait_recv()

        out = block(0, k)

        @pl.when(s > 0)
        def _():
            d_out[0, k] = out
            chain_copy(0, k, up).start()

    def partial(u, kind, e):
        q = e // PER_PART
        col = pl.multiple_of((e % PER_PART) * SHARD, SHARD)
        left_side = h_diag if kind == 0 else p_diag
        right_side = d_in if kind == 0 else x_fold
        rows = CHUNKS * TILE
        lane = pl.multiple_of(q * RANK, RANK)
        lhs = left_side[u, :, :, pl.ds(lane, RANK)].reshape(rows, RANK)
        rhs = right_side[u, :, :, pl.ds(col, SHARD)].reshape(rows, SHARD)
        return lax.dot_general(lhs, rhs, TN, preferred_element_type=F32)

    def pair_copy(u, kind):
        return copy(pair_out.at[u, kind], pair_in.at[u, kind], pair_s.at[u, kind], pair_r.at[u, kind], sib)

    def ring_copy(u, kind, slot, dev):
        return copy(
            ring_out.at[u, kind, slot], ring_in.at[u, kind, slot], ring_s.at[u, kind, slot], ring_r.at[u, kind, slot], dev
        )

    def gradients(u):
        for kind in (0, 1):
            def theirs(i, carry):
                pair_out[u, kind, i] = partial(u, kind, 2 * i + 1 - c).astype(BF16)
                return carry

            lax.fori_loop(0, N_X, theirs, 0)
            pair_copy(u, kind).start()
        for kind in (0, 1):
            def ours(i, carry):
                keep[u, kind, i] = partial(u, kind, 2 * i + c)
                return carry

            lax.fori_loop(0, N_X, ours, 0)
        ways = ((dev_right, right, dev_left, left), (dev_left, left, dev_right, right))
        for kind in (0, 1):
            ahead, ahead_x, behind, behind_x = ways[kind]
            pair_copy(u, kind).wait_recv()
            keep[u, kind] = keep[u, kind] + pair_in[u, kind].astype(F32)
            ring_out[u, kind, 0] = keep[u, kind, far].astype(BF16)
            ring_copy(u, kind, 0, ahead).start()
            ring_out[u, kind, 1] = keep[u, kind, behind_x].astype(BF16)
            ring_copy(u, kind, 1, behind).start()
        for kind in (0, 1):
            ahead, ahead_x, behind, behind_x = ways[kind]
            ring_copy(u, kind, 0, behind).wait_recv()
            ring_out[u, kind, 2] = (keep[u, kind, ahead_x] + ring_in[u, kind, 0].astype(F32)).astype(BF16)
            ring_copy(u, kind, 2, ahead).start()

    def collect(u):
        ways = ((dev_right, dev_left), (dev_left, dev_right))
        squares = jnp.zeros((1, 1), F32)
        for kind in (0, 1):
            ahead, behind = ways[kind]
            ring_copy(u, kind, 1, ahead).wait_recv()
            ring_copy(u, kind, 2, behind).wait_recv()
            grad = keep[u, kind, x] + ring_in[u, kind, 1].astype(F32) + ring_in[u, kind, 2].astype(F32)
            squares = squares + jnp.sum(jnp.sum(grad * grad, axis=0, keepdims=True), axis=1, keepdims=True)
            if kind == 0:
                grad_b[u] = grad
            else:
                grad_a[u] = grad.T
        return squares

    prepare(1)

    @pl.when(first)
    def _():
        window[0] = cot[...]

        def arrive(i, carry):
            copy(cot, window.at[i], cot_s, cot_r.at[i], sib).wait_recv()
            return carry

        lax.fori_loop(1, N_SECTION, arrive, 0)

        def tile(q, at, m):
            column = (q * WIDE + at) // RANK
            base, place = column // 5 * 4, column % 5
            value = None
            if place < 4:
                value = window[base + place, pl.ds(pl.multiple_of(m * TILE, TILE), TILE), :RANK].astype(F32)
            if place > 0:
                other = window[base + place - 1, pl.ds(pl.multiple_of(m * TILE, TILE), TILE), RANK:].astype(F32)
                value = other if value is None else value + other
            return value

        def micro(m, carry):
            refold(lambda q, at: tile(q, at, m), 1, d_in, m)
            return carry

        lax.fori_loop(0, MICRO, micro, 0)

    @pl.when(s >= LATE)
    def _():
        fold_stash(0)
        prepare(0)

    lag = jnp.where(s < LATE, CHUNKS, jnp.minimum(CHUNKS, LAG * (N_SECTION - 1 - s)))

    def tick(t, carry):
        upper(t)

        @pl.when(t >= lag)
        def _():
            lower(t - lag)

        return carry

    lax.fori_loop(0, CHUNKS, tick, 0)

    @pl.when(s < LATE)
    def _():
        fold_stash(0)
        prepare(0)
        gradients(1)

    def rest(k, carry):
        lower(k)
        return carry

    lax.fori_loop(CHUNKS - lag, CHUNKS, rest, 0)

    @pl.when(s >= LATE)
    def _():
        gradients(1)

    gradients(0)
    squares = collect(1) + collect(0)

    mine = jnp.broadcast_to(squares, (8, 128))

    @pl.when(s > 0)
    def _():
        norm_out[...] = mine
        up_copy = copy(norm_out, norm_in.at[s], nrm_s, nrm_r.at[s], home)
        up_copy.start()
        back = copy(lane_out, tot_in, lan_s.at[0], tot_r, home)
        back.wait_recv()
        total[...] = tot_in[...]
        up_copy.wait_send()

    @pl.when(first)
    def _():
        norm_in[0] = mine

        def arrive(i, carry):
            copy(norm_out, norm_in.at[i], nrm_s, nrm_r.at[i], sib).wait_recv()
            return carry

        lax.fori_loop(1, N_SECTION, arrive, 0)
        lane_out[...] = jnp.sum(norm_in[...], axis=0)

        def share(i):
            return copy(lane_out, lane_in.at[i], lan_s.at[i], lan_r.at[i], (0, lax.rem(d + i, N_DP)))

        for i in range(1, N_DP):
            share(i).start()
        for i in range(1, N_DP):
            share(i).wait_recv()
        lane_in[0] = lane_out[...]
        value = jnp.sum(lane_in[...], axis=0)
        total[...] = value
        norm_out[...] = value

        def send(i, carry):
            copy(norm_out, tot_in, tot_s.at[i], tot_r, (i, d)).start()
            return carry

        lax.fori_loop(1, N_SECTION, send, 0)

        def sent(i, carry):
            copy(norm_out, tot_in, tot_s.at[i], tot_r, (i, d)).wait_send()
            return carry

        lax.fori_loop(1, N_SECTION, sent, 0)
        for i in range(1, N_DP):
            share(i).wait_send()

    @pl.when(s > 0)
    def _():
        copy(cot, window.at[s], cot_s, cot_r.at[s], home).wait_send()

    for u in (0, 1):
        for one in gather_sends(u):
            one.wait_send()
        for kind in (0, 1):
            pair_copy(u, kind).wait_send()
            for slot in range(3):
                ring_copy(u, kind, slot, sib).wait_send()

    @pl.when(s < N_SECTION - 1)
    def _():
        def sent(k, carry):
            chain_copy(1, k, down).wait_send()
            return carry

        lax.fori_loop(0, CHUNKS, sent, 0)

    @pl.when(s > 0)
    def _():
        def sent(k, carry):
            chain_copy(0, k, up).wait_send()
            return carry

        lax.fori_loop(0, CHUNKS, sent, 0)


def chain(stash, cot, a_param, b_param):
    dma = pltpu.SemaphoreType.DMA
    vmem = pl.BlockSpec(memory_space=pltpu.VMEM)
    part = (2, 2, N_X, RANK, SHARD)
    return pl.pallas_call(
        chain_kernel,
        name="chain",
        out_shape=(
            jax.ShapeDtypeStruct((2, SHARD, RANK), F32),
            jax.ShapeDtypeStruct((2, RANK, SHARD), F32),
            jax.ShapeDtypeStruct((8, 128), F32),
        ),
        in_specs=[vmem] * 4,
        out_specs=(vmem,) * 3,
        scratch_shapes=[
            pltpu.VMEM((2, WIDE, FOLD * RANK), BF16),
            pltpu.VMEM((2, FOLD * RANK, WIDE), BF16),
            pltpu.VMEM((2, CHUNKS, TILE, WIDE), BF16),
            pltpu.VMEM((2, CHUNKS, TILE, WIDE), BF16),
            pltpu.VMEM((2, CHUNKS, TILE, WIDE), BF16),
            pltpu.VMEM((2, CHUNKS, TILE, RANK), F32),
            pltpu.VMEM((2, CHUNKS, TILE, RANK), F32),
            pltpu.VMEM((2, CHUNKS, TILE, FOLD * RANK), BF16),
            pltpu.VMEM((2, CHUNKS, TILE, FOLD * RANK), BF16),
            pltpu.VMEM((N_SECTION, MICRO * TILE, 2 * RANK), BF16),
            pltpu.VMEM(part, F32),
            pltpu.VMEM(part, BF16),
            pltpu.VMEM(part, BF16),
            pltpu.VMEM((2, 2, 3, RANK, SHARD), BF16),
            pltpu.VMEM((2, 2, 3, RANK, SHARD), BF16),
            pltpu.VMEM((8, 128), F32),
            pltpu.VMEM((N_SECTION, 8, 128), F32),
            pltpu.VMEM((8, 128), F32),
            pltpu.VMEM((N_DP, 8, 128), F32),
            pltpu.VMEM((8, 128), F32),
            dma((2, 14)), dma((2, 14)),
            dma((2, CHUNKS)), dma((2, CHUNKS)),
            dma, dma((N_SECTION,)),
            dma((2, 2)), dma((2, 2)),
            dma((2, 2, 3)), dma((2, 2, 3)),
            dma, dma((N_SECTION,)),
            dma((N_DP,)), dma((N_DP,)),
            dma((N_SECTION,)), dma,
        ],
        compiler_params=pltpu.CompilerParams(collective_id=0, has_side_effects=True, vmem_limit_bytes=58 << 20),
    )(stash, cot, a_param, b_param)


def adam_update(param, moment, second, grad, clip_factor):
    scaled = clip_factor * grad
    moment_new = beta_one * moment + (1.0 - beta_one) * scaled
    second_new = beta_two * second + (1.0 - beta_two) * scaled * scaled
    param_new = param - learning_rate * moment_new / (jnp.sqrt(second_new) + adam_epsilon)
    return (param_new, moment_new, second_new)


def shards(stash, cotangent, a_param, a_moment, a_second, b_param, b_moment, b_second):
    position = lax.axis_index("section")
    flat = cotangent.reshape(MICRO * TILE, D // N_SECTION)
    cot = lax.dynamic_update_slice(
        jnp.zeros((MICRO * TILE, 2 * RANK), BF16), flat, (0, 32 * lax.rem(position, 4))
    )
    grad_a, grad_b, total = chain(stash[:, 0], cot, a_param[:, 0], b_param[:, 0])
    grad_norm = jnp.sqrt(total[0, 0])
    entries = 4 * N_SECTION * D * RANK
    clip_factor = jnp.minimum(1.0, 0.5 * math.sqrt(entries) / grad_norm)
    a_new, a_moment_new, a_second_new = adam_update(a_param, a_moment, a_second, grad_a[:, None], clip_factor)
    b_new, b_moment_new, b_second_new = adam_update(b_param, b_moment, b_second, grad_b[:, None], clip_factor)
    return (a_new, a_moment_new, a_second_new, b_new, b_moment_new, b_second_new, grad_norm)


def solution(mesh):
    return jax.shard_map(
        shards,
        mesh=mesh,
        in_specs=(
            P(None, "section", None, "dp", None),
            P(None, "dp", "section"),
            P(None, "section", "dp", None),
            P(None, "section", "dp", None),
            P(None, "section", "dp", None),
            P(None, "section", None, "dp"),
            P(None, "section", None, "dp"),
            P(None, "section", None, "dp"),
        ),
        out_specs=(
            P(None, "section", "dp", None),
            P(None, "section", "dp", None),
            P(None, "section", "dp", None),
            P(None, "section", None, "dp"),
            P(None, "section", None, "dp"),
            P(None, "section", None, "dp"),
            P(),
        ),
        check_vma=False,
    )
```

time: 1470 us -> 360 us (0.24)
  waiting for transfers between devices: 501 us -> 0 us
  local copies, waits for them, and re-layouts: 427 us -> 3.28 us
  Pallas kernels: 0 us -> 349 us
  starting transfers between devices: 241 us -> 0 us
  other arithmetic: 116 us -> 4.57 us
  blocking collectives: 78.7 us -> 0 us
  matrix products: 74.9 us -> 0 us
    pallas_call x0 -> x1, Pallas kernels: none -> 349 us  [chain(): pl.pallas_call(chain_kernel, name='chain', out_shape=(jax.ShapeDtypeStruc...]
    ppermute x78 -> x0, starting transfers between devices: 240 us -> none  [from_behind(): lax.ppermute(value, axis, [(source, source + steps) for source in range(i...]
    ppermute x78 -> x0, waiting for transfers between devices: 221 us -> none  [from_behind(): lax.ppermute(value, axis, [(source, source + steps) for source in range(i...]
    all_gather x3 -> x0, waiting for transfers between devices: 163 us -> none  [the longest x1 112 us: shards(): first_deltas = lax.all_gather(cotangent, 'section', axis=2, tiled=True)]
    slice x250 -> x1, local copies, waits for them, and re-layouts: 148 us -> 1.29 us  [shards(): grad_norm = jnp.sqrt(total[0, 0])]
    scatter x163 -> x0, local copies, waits for them, and re-layouts: 144 us -> none  [place_row(): store.at[which]]
    unnamed x6 -> x0, waiting for transfers between devices: 81.8 us -> none
    psum x1 -> x0, blocking collectives: 78.7 us -> none  [shards(): square_total = lax.psum(local_squares, ('section', 'dp'))]
  transfers between devices with their start and end apart: 83 -> 0, of which waited for: 38 -> 0; matrix products, arithmetic and copies ran while one was open for 20% -> 0% of each run, Pallas kernels for 0% -> 0%
where the time goes in v1:
time: 360 us
  Pallas kernels  349 us (97%)
  other arithmetic  4.57 us (1%)
    pallas_call x1, Pallas kernels, chain(): pl.pallas_call(chain_kernel, name='chain', out_shape=(jax.ShapeDtypeStruc...  349 us

profile of v1, /device:TPU:1, one launch (start us, length us, event | category | flops | bytes accessed | tf_op | source)
XLA Modules:
  0.0 359.8 jit_solution(3508912464597711268)
XLA Ops:
  0.6 0.0 copy-start
  0.6 0.0 copy-start.2
  0.7 0.0 copy-start.3
  0.7 1.3 dynamic_update_slice.3.cot
  2.0 0.0 copy-start.7
  2.0 0.6 copy-done.7
  2.6 349.3 %chain.1 = (f32[2,640,128]{2,1,0:T(8,128)}, f32[2,128,640]{2,1,0:T(8,128)}, f32[8,128]{1,0:T(8,128)}) custom-call(bf16[2,8,16,5120]{3,2,1,0:T(8,128)(2,1)} %bitcast.85, bf16[128,256]{1,0:T(8,128)(2,1)} %copy-done.7, f32[2,640,128]{2,1,0:T(8,128)} %bitcast.87, f32[2,128,640]{2,1,0:T(8,128)} %bitcast.86), custom_call_target="tpu_custom_call" | custom-call | tf_op jit(solution)/shard_map/chain/pallas_call | solution.py:509
  352.0 0.0 copy-start.1
  352.0 0.0 copy-start.4
  352.0 1.3 slice.3
  354.0 0.0 copy-done
  354.0 0.0 copy-done.2
  354.0 0.0 copy-done.3
  354.0 0.0 copy-start.5
  354.0 0.0 copy-start.6
  354.1 2.9 fusion.8
  356.9 0.0 copy-done.1
  356.9 0.0 copy-done.4
  356.9 0.0 copy-done.5
  356.9 0.0 copy-done.6
  357.0 1.7 fusion.9
  (1 shorter events, 0.0 us)
Async XLA Ops:
  0.6 353.4 %copy-start = (f32[2,1,128,640]{3,2,1,0:T(8,128)S(1)}, f32[2,1,128,640]{3,2,1,0:T(8,128)}, u32[]{:S(2)}) copy-start(f32[2,1,128,640]{3,2,1,0:T(8,128)} %param.13) | copy-start | bytes 1966084
  0.6 353.4 %copy-start.2 = (f32[2,1,128,640]{3,2,1,0:T(8,128)S(1)}, f32[2,1,128,640]{3,2,1,0:T(8,128)}, u32[]{:S(2)}) copy-start(f32[2,1,128,640]{3,2,1,0:T(8,128)} %param.15) | copy-start | bytes 1966084
  0.7 353.4 %copy-start.3 = (f32[2,1,128,640]{3,2,1,0:T(8,128)S(1)}, f32[2,1,128,640]{3,2,1,0:T(8,128)}, u32[]{:S(2)}) copy-start(f32[2,1,128,640]{3,2,1,0:T(8,128)} %param.14) | copy-start | bytes 1966084
  2.0 0.6 copy-start.7
  352.0 5.0 %copy-start.1 = (f32[2,1,640,128]{3,2,1,0:T(8,128)S(1)}, f32[2,1,640,128]{3,2,1,0:T(8,128)}, u32[]{:S(2)}) copy-start(f32[2,1,640,128]{3,2,1,0:T(8,128)} %param.10) | copy-start | bytes 1966084
  352.0 5.0 %copy-start.4 = (f32[2,1,640,128]{3,2,1,0:T(8,128)S(1)}, f32[2,1,640,128]{3,2,1,0:T(8,128)}, u32[]{:S(2)}) copy-start(f32[2,1,640,128]{3,2,1,0:T(8,128)} %param.12) | copy-start | bytes 1966084
  354.0 2.9 copy-start.5
  354.0 2.9 copy-start.6

commit v2 on v1

v2 whole, which is shorter than its diff:
```python
import functools
import math

import jax
import jax.numpy as jnp
from jax import lax
from jax.experimental import pallas as pl
from jax.experimental.pallas import tpu as pltpu
from jax.sharding import PartitionSpec as P

beta_one = 0.9
beta_two = 0.95
learning_rate = 0.01
adam_epsilon = 1e-08
norm_epsilon = 1e-06

MESH = pl.DeviceIdType.MESH
F32 = jnp.float32
BF16 = jnp.bfloat16

N_SECTION = 32
N_Z = 8
N_X = 4
N_DP = 8
D = 5120
RANK = 128
MICRO = 8
TILE = 16
SHARD = D // N_DP
FOLD = 4
ROWS = TILE // FOLD
CHUNKS = MICRO * FOLD
WIDE = D // FOLD
PER_PART = WIDE // SHARD
TEAM = 4
TEAMS = N_SECTION // TEAM
SHARE = CHUNKS // TEAM
HALF = SHARE // 2
INPUTS, GATES, OPEN, LATE = 1, 2, 3, 7
BACK = 6
EARLY = 3
LAG = 5

NT = (((1,), (1,)), ((), ()))
TN = (((0,), (0,)), ((), ()))


def row_group():
    return lax.broadcasted_iota(jnp.int32, (TILE, RANK), 0) // ROWS


def spread(value):
    step = TILE // 2
    while step >= ROWS:
        value = value + pltpu.roll(value, step, 0)
        step //= 2
    return value


def diagonal(value, group):
    return jnp.concatenate([jnp.where(group == q, value, 0.0) for q in range(FOLD)], axis=1)


def chain_kernel(
    stash, cot, a_param, b_param,
    grad_a, grad_b, total,
    w_b, w_a, x_fold, gates_own, hid, d_in, p_in, x_slot, gates_slot, d_slot, p_slot, d_out, window, mask,
    keep, pair_out, pair_in, ring_out, ring_in, norm_out, norm_in, lane_out, lane_in, tot_in,
    zw_s, zw_r, gat_s, gat_r, dx_s, dx_r, dg_s, dg_r, rd_s, rd_r, rp_s, rp_r, ch_s, ch_r, cot_s, cot_r,
    pair_s, pair_r, ring_s, ring_r, nrm_s, nrm_r, lan_s, lan_r, tot_s, tot_r,
):
    s = lax.axis_index("section")
    d = lax.axis_index("dp")
    x = d // 2
    c = d % 2
    right = lax.rem(x + 1, N_X)
    left = lax.rem(x + N_X - 1, N_X)
    far = lax.rem(x + 2, N_X)
    sib = (s, 2 * x + 1 - c)
    dev_right = (s, 2 * right + c)
    dev_left = (s, 2 * left + c)
    team = s // TEAM
    own = s % TEAM
    odd = team % 2
    base = team * TEAM

    def slot_of(i):
        return i + odd * (TEAM - 1 - 2 * i)

    slot = slot_of(own)
    mine = slot * SHARE
    first = team == 0
    last = team == TEAMS - 1
    down = (jnp.minimum(base + TEAM + TEAM - 1 - own, N_SECTION - 1), d)
    up = (jnp.maximum(base - 1 - own, 0), d)
    home = (0, d)
    group = row_group()

    def mate(j):
        return lax.rem(own + j, TEAM)

    def copy(src, dst, ssem, rsem, dev):
        return pltpu.make_async_remote_copy(
            src_ref=src, dst_ref=dst, send_sem=ssem, recv_sem=rsem, device_id=dev, device_id_type=MESH
        )

    def repeat(low, high, body):
        def step(i, carry):
            body(i)
            return carry

        lax.fori_loop(low, high, step, 0)

    bar = pltpu.get_barrier_semaphore()

    def hello(dev):
        pl.semaphore_signal(bar, inc=1, device_id=dev, device_id_type=MESH)

    hello(sib)
    hello(dev_right)
    hello(dev_left)
    for j in range(1, TEAM):
        hello((base + mate(j), d))

    @pl.when(team > 0)
    def _():
        hello(up)

    @pl.when(team < TEAMS - 1)
    def _():
        hello(down)

    @pl.when(s > 0)
    def _():
        hello(home)

    @pl.when(first)
    def _():
        repeat(1, N_SECTION, lambda i: hello((lax.rem(s + i, N_SECTION), d)))

    @pl.when(s == 0)
    def _():
        repeat(1, N_DP, lambda i: hello((0, lax.rem(d + i, N_DP))))

    def b_slice(u, i, e):
        row = pl.multiple_of((e % PER_PART) * SHARD, SHARD)
        col = pl.multiple_of((e // PER_PART) * RANK, RANK)
        return w_b.at[u, i, pl.ds(row, SHARD), pl.ds(col, RANK)]

    def a_slice(u, i, e):
        row = pl.multiple_of((e // PER_PART) * RANK, RANK)
        col = pl.multiple_of((e % PER_PART) * SHARD, SHARD)
        return w_a.at[u, i, pl.ds(row, RANK), pl.ds(col, SHARD)]

    def piece(u, i, e, kind):
        return b_slice(u, i, e) if kind == 0 else a_slice(u, i, e)

    def own_weights(u):
        b_slice(u, own, d)[...] = b_param[u].T.astype(BF16)
        a_slice(u, own, d)[...] = a_param[u].T.astype(BF16)

    def refold(get, put):
        for at in range(0, WIDE, RANK):
            parts = [get(q, at) for q in range(FOLD)]
            outs = [None] * FOLD
            for q in range(FOLD):
                for j in range(FOLD):
                    turn = (ROWS * (q - j)) % TILE
                    moved = parts[q] if turn == 0 else pltpu.roll(parts[q], turn, 0)
                    outs[j] = moved if q == 0 else jnp.where(group == q, moved, outs[j])
            for j in range(FOLD):
                put(j, at, outs[j].astype(BF16))

    def fold_stash(u):
        def micro(m):
            def put(j, at, value):
                x_fold[u, m * FOLD + j, :, at : at + RANK] = value

            refold(lambda q, at: stash[u, m, :, q * WIDE + at : q * WIDE + at + RANK].astype(F32), put)

        repeat(0, MICRO, micro)

    own_weights(1)
    own_weights(0)
    for q in range(FOLD):
        mask[q] = jnp.where(group == q, 1.0, 0.0).astype(BF16)

    pl.semaphore_wait(
        bar,
        6
        + (team > 0).astype(jnp.int32)
        + (team < TEAMS - 1).astype(jnp.int32)
        + jnp.where(first, TEAM - 1, TEAM)
        + jnp.where(s == 0, N_SECTION + N_DP - 2, 0),
    )

    def team_weights(u, j, kind):
        i = mate(j)
        ref = piece(u, own, d, kind)
        return copy(ref, ref, zw_s.at[u, kind, i], zw_r.at[u, kind, own], (base + i, d))

    def team_weights_in(u, j, kind):
        i = mate(j)
        ref = piece(u, i, d, kind)
        return copy(ref, ref, zw_s.at[u, kind, i], zw_r.at[u, kind, i], (base + i, d))

    def share_x(u, j):
        i = mate(j)
        src = x_fold.at[u, pl.ds(slot_of(i) * SHARE, SHARE)]
        return copy(src, x_slot.at[u, own], dx_s.at[u, i], dx_r.at[u, own], (base + i, d))

    def share_x_in(u, j):
        i = mate(j)
        src = x_fold.at[u, pl.ds(mine, SHARE)]
        return copy(src, x_slot.at[u, i], dx_s.at[u, i], dx_r.at[u, i], (base + i, d))

    def share_gates(u, j):
        i = mate(j)
        src = gates_own.at[u, pl.ds(slot_of(i) * SHARE, SHARE)]
        return copy(src, gates_slot.at[u, own], dg_s.at[u, i], dg_r.at[u, own], (base + i, d))

    def share_gates_in(u, j):
        i = mate(j)
        src = gates_own.at[u, pl.ds(mine, SHARE)]
        return copy(src, gates_slot.at[u, i], dg_s.at[u, i], dg_r.at[u, i], (base + i, d))

    def back_d(u, j, h):
        i = mate(j)
        src = d_slot.at[u, i, pl.ds(h * HALF, HALF)]
        dst = d_in.at[u, pl.ds(mine + h * HALF, HALF)]
        return copy(src, dst, rd_s.at[u, i, h], rd_r.at[u, own, h], (base + i, d))

    def back_d_in(u, j, h):
        i = mate(j)
        src = d_slot.at[u, i, pl.ds(h * HALF, HALF)]
        dst = d_in.at[u, pl.ds(slot_of(i) * SHARE + h * HALF, HALF)]
        return copy(src, dst, rd_s.at[u, i, h], rd_r.at[u, i, h], (base + i, d))

    def back_p(u, j, h):
        i = mate(j)
        src = p_slot.at[u, i, pl.ds(h * HALF, HALF)]
        dst = p_in.at[u, pl.ds(mine + h * HALF, HALF)]
        return copy(src, dst, rp_s.at[u, i, h], rp_r.at[u, own, h], (base + i, d))

    def back_p_in(u, j, h):
        i = mate(j)
        src = p_slot.at[u, i, pl.ds(h * HALF, HALF)]
        dst = p_in.at[u, pl.ds(slot_of(i) * SHARE + h * HALF, HALF)]
        return copy(src, dst, rp_s.at[u, i, h], rp_r.at[u, i, h], (base + i, d))

    for kind in (0, 1):
        for j in range(1, TEAM):
            team_weights(1, j, kind).start()

    def cot_copy(r):
        src = cot.at[pl.ds(pl.multiple_of(r * 2 * TILE, 2 * TILE), 2 * TILE)]
        return copy(src, window.at[s], cot_s.at[r], cot_r.at[s], (r, d))

    def to_first(body):
        def one(r):
            @pl.when(s != r)
            def _():
                body(r)

        repeat(0, TEAM, one)

    to_first(lambda r: cot_copy(r).start())

    def gather_copy(u, i, at, xs, cs, kind, dev):
        ref = piece(u, i, 2 * xs + cs, kind)
        return copy(ref, ref, gat_s.at[u, i, at], gat_r.at[u, i, at], dev)

    def gather_sends(u, i):
        return [
            gather_copy(u, i, 0, x, c, 0, dev_right),
            gather_copy(u, i, 1, x, c, 1, dev_right),
            gather_copy(u, i, 2, x, c, 0, dev_left),
            gather_copy(u, i, 3, x, c, 1, dev_left),
            gather_copy(u, i, 4, left, c, 0, dev_right),
            gather_copy(u, i, 5, right, c, 1, dev_left),
        ] + [
            gather_copy(u, i, 6 + 2 * n + kind, xs, c, kind, sib)
            for n, xs in enumerate((x, left, right, far))
            for kind in (0, 1)
        ]

    def gather_recvs(u, i):
        return [
            gather_copy(u, i, 0, left, c, 0, dev_left),
            gather_copy(u, i, 1, left, c, 1, dev_left),
            gather_copy(u, i, 2, right, c, 0, dev_right),
            gather_copy(u, i, 3, right, c, 1, dev_right),
            gather_copy(u, i, 4, far, c, 0, dev_left),
            gather_copy(u, i, 5, far, c, 1, dev_right),
        ] + [
            gather_copy(u, i, 6 + 2 * n + kind, xs, 1 - c, kind, sib)
            for n, xs in enumerate((x, left, right, far))
            for kind in (0, 1)
        ]

    def gather_open(u, i):
        out = gather_sends(u, i)
        for n in (0, 3, 1, 2, 6, 7):
            out[n].start()

    def gather_close(u, i):
        out, arr = gather_sends(u, i), gather_recvs(u, i)
        arr[0].wait_recv()
        out[4].start()
        out[8].start()
        arr[3].wait_recv()
        out[5].start()
        out[11].start()
        arr[1].wait_recv()
        out[9].start()
        arr[2].wait_recv()
        out[10].start()
        arr[4].wait_recv()
        out[12].start()
        arr[5].wait_recv()
        out[13].start()
        for n in range(6, 14):
            arr[n].wait_recv()

    def gather_next(u, j):
        for kind in (0, 1):
            team_weights_in(u, j, kind).wait_recv()
        gather_open(u, mate(j))

    def gates(u):
        flat = MICRO * TILE
        pre = jnp.zeros((flat, RANK), F32)
        squares = jnp.zeros((flat, 1), F32)
        for e in range(N_DP):
            part = stash[u, :, :, e * SHARD : (e + 1) * SHARD].reshape(flat, SHARD)
            wide = part.astype(F32)
            squares = squares + jnp.sum(wide * wide, axis=1, keepdims=True)
            q, off = e // PER_PART, (e % PER_PART) * SHARD
            pre = pre + lax.dot_general(
                part, w_a[u, own, q * RANK : (q + 1) * RANK, off : off + SHARD], NT, preferred_element_type=F32
            )
        inv = lax.rsqrt(squares * (1.0 / D) + norm_epsilon)
        pre = pre * inv
        sig = 1.0 / (1.0 + jnp.exp(-pre))
        hidden = pre * sig
        turn = sig * (1.0 + pre * (1.0 - sig)) * inv
        lean = pre * inv * (1.0 / D)
        for m in range(MICRO):
            for j in range(FOLD):
                here = m * FOLD + j
                rows = slice(m * TILE, (m + 1) * TILE)
                gates_own[u, here, 0] = spread(jnp.where(group == j, turn[rows], 0.0))
                gates_own[u, here, 1] = spread(jnp.where(group == j, lean[rows], 0.0))
                hid[u, here] = spread(jnp.where(group == j, hidden[rows], 0.0)).astype(BF16)

    def give_x(u):
        for j in range(1, TEAM):
            share_x(u, j).start()

        def keep_own(k):
            x_slot[u, own, k] = x_fold[u, mine + k]

        repeat(0, SHARE, keep_own)

    def give_gates(u):
        gates(u)
        for j in range(1, TEAM):
            share_gates(u, j).start()

        def keep_own(k):
            gates_slot[u, own, k] = gates_own[u, mine + k]

        repeat(0, SHARE, keep_own)

    def take(u):
        for j in range(1, TEAM):
            share_x_in(u, j).wait_recv()
            share_gates_in(u, j).wait_recv()

    gather_open(1, own)
    fold_stash(1)
    gather_close(1, own)
    give_gates(1)
    repeat(1, TEAM, lambda j: gather_next(1, j))
    give_x(1)

    @pl.when(first)
    def _():
        window[s] = cot[pl.ds(pl.multiple_of(s * 2 * TILE, 2 * TILE), 2 * TILE), :]

        def arrive(i):
            copy(
                cot.at[pl.ds(0, 2 * TILE)], window.at[lax.rem(s + i, N_SECTION)], cot_s.at[0],
                cot_r.at[lax.rem(s + i, N_SECTION)], sib,
            ).wait_recv()

        repeat(1, N_SECTION, arrive)

        def tile(q, at, m):
            column = (q * WIDE + at) // RANK
            start, place = column // 5 * 4, column % 5
            rows = slice(m * TILE, (m + 1) * TILE)
            value = None
            if place < 4:
                value = window[start + place, rows, :RANK].astype(F32)
            if place > 0:
                other = window[start + place - 1, rows, RANK:].astype(F32)
                value = other if value is None else value + other
            return value

        for m in range(2):
            def put(j, at, value):
                d_slot[1, 0, m * FOLD + j, :, at : at + RANK] = value

            refold(lambda q, at: tile(q, at, m), put)

    repeat(1, TEAM, lambda j: gather_close(1, mate(j)))
    for kind in (0, 1):
        for j in range(1, TEAM):
            team_weights(0, j, kind).start()
    gather_open(0, own)
    take(1)

    def lower_inputs():
        fold_stash(0)
        give_x(0)

    def lower_gates():
        gather_close(0, own)
        give_gates(0)

    def lower_open():
        repeat(1, TEAM, lambda j: gather_next(0, j))

    def lower_close():
        repeat(1, TEAM, lambda j: gather_close(0, mate(j)))

    pl.when(team >= INPUTS)(lower_inputs)
    pl.when(team >= GATES)(lower_gates)
    pl.when(team >= OPEN)(lower_open)

    @pl.when(team >= LATE)
    def _():
        lower_close()
        take(0)

    def chain_copy(u, k, dev):
        place = d_slot.at[1, 0, k] if u == 1 else d_slot.at[0, TEAM - 1, k]
        return copy(d_out.at[u, k], place, ch_s.at[u, k], ch_r.at[u, k], dev)

    def block(u, i, k, incoming):
        wide = jnp.dot(incoming, w_b[u, i], preferred_element_type=F32)
        picked = jnp.where(group == 0, wide[:, :RANK], 0.0)
        for q in range(1, FOLD):
            picked = jnp.where(group == q, wide[:, q * RANK : (q + 1) * RANK], picked)
        grad_hidden = spread(picked)
        small = (grad_hidden * gates_slot[u, i, k, 0]).astype(BF16)
        p_slot[u, i, k] = small
        grad_pre = small.astype(F32)
        shift = jnp.sum(grad_pre * gates_slot[u, i, k, 1], axis=1, keepdims=True)
        diag = diagonal(grad_pre, group).astype(BF16)
        back = jnp.dot(diag, w_a[u, i], preferred_element_type=F32)
        return (incoming.astype(F32) + back - x_slot[u, i, k].astype(F32) * shift).astype(BF16)

    def walk(u, k):
        order = list(range(TEAM)) if u == 1 else list(range(TEAM))[::-1]
        value = d_slot[u, order[0], k]
        for n, i in enumerate(order):
            value = block(u, i, k, value)
            if n < TEAM - 1:
                d_slot[u, order[n + 1], k] = value
        return value

    def upper(k):
        @pl.when(team > 0)
        def _():
            chain_copy(1, k, up).wait_recv()

        out = walk(1, k)

        @pl.when(last)
        def _():
            d_slot[0, TEAM - 1, k] = out

        @pl.when(team < TEAMS - 1)
        def _():
            d_out[1, k] = out
            chain_copy(1, k, down).start()

    def give_back(u, h):
        for j in range(1, TEAM):
            back_d(u, j, h).start()
            back_p(u, j, h).start()

    def lower(k):
        @pl.when(team < TEAMS - 1)
        def _():
            chain_copy(0, k, down).wait_recv()

        out = walk(0, k)

        @pl.when(team > 0)
        def _():
            d_out[0, k] = out
            chain_copy(0, k, up).start()

        @pl.when(first & (k == HALF - 1))
        def _():
            give_back(0, 0)

    def partial(u, kind, e):
        q = e // PER_PART
        col = pl.multiple_of((e % PER_PART) * SHARD, SHARD)
        rows = CHUNKS * TILE
        small = hid[u] if kind == 0 else p_in[u]
        right_side = d_in if kind == 0 else x_fold
        lhs = (small * mask[q][None]).reshape(rows, RANK)
        rhs = right_side[u, :, :, pl.ds(col, SHARD)].reshape(rows, SHARD)
        return lax.dot_general(lhs, rhs, TN, preferred_element_type=F32)

    def pair_copy(u, kind):
        return copy(pair_out.at[u, kind], pair_in.at[u, kind], pair_s.at[u, kind], pair_r.at[u, kind], sib)

    def ring_copy(u, kind, at, dev):
        return copy(ring_out.at[u, kind, at], ring_in.at[u, kind, at], ring_s.at[u, kind, at], ring_r.at[u, kind, at], dev)

    def gradients(u):
        def keep_own(k):
            d_in[u, mine + k] = d_slot[u, own, k]
            p_in[u, mine + k] = p_slot[u, own, k]

        repeat(0, SHARE, keep_own)
        for j in range(1, TEAM):
            for h in (0, 1):
                back_d_in(u, j, h).wait_recv()
                back_p_in(u, j, h).wait_recv()
        for kind in (0, 1):
            def theirs(i):
                pair_out[u, kind, i] = partial(u, kind, 2 * i + 1 - c).astype(BF16)

            repeat(0, N_X, theirs)
            pair_copy(u, kind).start()
        for kind in (0, 1):
            def ours(i):
                keep[kind, i] = partial(u, kind, 2 * i + c)

            repeat(0, N_X, ours)
        ways = ((dev_right, right, dev_left, left), (dev_left, left, dev_right, right))
        for kind in (0, 1):
            ahead, ahead_x, behind, behind_x = ways[kind]
            pair_copy(u, kind).wait_recv()
            keep[kind] = keep[kind] + pair_in[u, kind].astype(F32)
            ring_out[u, kind, 0] = keep[kind, far].astype(BF16)
            ring_copy(u, kind, 0, ahead).start()
            ring_out[u, kind, 1] = keep[kind, behind_x].astype(BF16)
            ring_copy(u, kind, 1, behind).start()
        for kind in (0, 1):
            ahead, ahead_x, behind, behind_x = ways[kind]
            ring_copy(u, kind, 0, behind).wait_recv()
            ring_out[u, kind, 2] = (keep[kind, ahead_x] + ring_in[u, kind, 0].astype(F32)).astype(BF16)
            ring_copy(u, kind, 2, ahead).start()
        squares = jnp.zeros((1, 1), F32)
        for kind in (0, 1):
            ahead, ahead_x, behind, behind_x = ways[kind]
            ring_copy(u, kind, 1, ahead).wait_recv()
            ring_copy(u, kind, 2, behind).wait_recv()
            grad = keep[kind, x] + ring_in[u, kind, 1].astype(F32) + ring_in[u, kind, 2].astype(F32)
            squares = squares + jnp.sum(jnp.sum(grad * grad, axis=0, keepdims=True), axis=1, keepdims=True)
            if kind == 0:
                grad_b[u] = grad
            else:
                grad_a[u] = grad.T
        norm_out[...] = norm_out[...] + jnp.broadcast_to(squares, (8, 128))

    norm_out[...] = jnp.zeros((8, 128), F32)

    lag = jnp.where(team < LATE, SHARE, jnp.minimum(SHARE, LAG * (TEAMS - 1 - team)))

    def tick(t):
        upper(t)

        @pl.when(t >= lag)
        def _():
            lower(t - lag)

    repeat(0, SHARE, tick)

    def back_upper():
        for h in (0, 1):
            give_back(1, h)

    pl.when(team < INPUTS)(lower_inputs)
    pl.when(team < GATES)(lower_gates)
    pl.when(team < OPEN)(lower_open)
    pl.when(team < LATE)(lower_close)
    pl.when(team < BACK)(back_upper)
    pl.when(team < EARLY)(lambda: gradients(1))
    pl.when(team < LATE)(lambda: take(0))
    repeat(SHARE - lag, SHARE, lower)
    pl.when(team >= BACK)(back_upper)
    pl.when(team > 0)(lambda: give_back(0, 0))
    give_back(0, 1)
    pl.when(team >= EARLY)(lambda: gradients(1))
    gradients(0)

    @pl.when(s > 0)
    def _():
        up_copy = copy(norm_out, norm_in.at[s], nrm_s, nrm_r.at[s], home)
        up_copy.start()
        copy(lane_out, tot_in, lan_s.at[0], tot_r, home).wait_recv()
        total[...] = tot_in[...]
        up_copy.wait_send()

    @pl.when(s == 0)
    def _():
        norm_in[0] = norm_out[...]
        repeat(1, N_SECTION, lambda i: copy(norm_out, norm_in.at[i], nrm_s, nrm_r.at[i], sib).wait_recv())
        lane_out[...] = jnp.sum(norm_in[...], axis=0)

        def share(i):
            return copy(lane_out, lane_in.at[i], lan_s.at[i], lan_r.at[i], (0, lax.rem(d + i, N_DP)))

        for i in range(1, N_DP):
            share(i).start()
        for i in range(1, N_DP):
            share(i).wait_recv()
        lane_in[0] = lane_out[...]
        value = jnp.sum(lane_in[...], axis=0)
        total[...] = value
        norm_out[...] = value
        repeat(1, N_SECTION, lambda i: copy(norm_out, tot_in, tot_s.at[i], tot_r, (i, d)).start())
        repeat(1, N_SECTION, lambda i: copy(norm_out, tot_in, tot_s.at[i], tot_r, (i, d)).wait_send())
        for i in range(1, N_DP):
            share(i).wait_send()

    to_first(lambda r: cot_copy(r).wait_send())
    for u in (0, 1):
        def sent(j):
            for one in gather_sends(u, mate(j)):
                one.wait_send()

        repeat(0, TEAM, sent)
        for kind in (0, 1):
            pair_copy(u, kind).wait_send()
            for at in range(3):
                ring_copy(u, kind, at, sib).wait_send()

        def given(j):
            for kind in (0, 1):
                team_weights(u, j, kind).wait_send()
            share_x(u, j).wait_send()
            share_gates(u, j).wait_send()
            for h in (0, 1):
                back_d(u, j, h).wait_send()
                back_p(u, j, h).wait_send()

        repeat(1, TEAM, given)

    @pl.when(team < TEAMS - 1)
    def _():
        repeat(0, SHARE, lambda k: chain_copy(1, k, down).wait_send())

    @pl.when(team > 0)
    def _():
        repeat(0, SHARE, lambda k: chain_copy(0, k, up).wait_send())


def chain(stash, cot, a_param, b_param):
    dma = pltpu.SemaphoreType.DMA
    vmem = pl.BlockSpec(memory_space=pltpu.VMEM)
    part = (2, 2, N_X, RANK, SHARD)
    own_rows = (2, CHUNKS, TILE)
    slot_rows = (2, TEAM, SHARE, TILE)
    return pl.pallas_call(
        chain_kernel,
        name="chain",
        out_shape=(
            jax.ShapeDtypeStruct((2, SHARD, RANK), F32),
            jax.ShapeDtypeStruct((2, RANK, SHARD), F32),
            jax.ShapeDtypeStruct((8, 128), F32),
        ),
        in_specs=[vmem] * 4,
        out_specs=(vmem,) * 3,
        scratch_shapes=[
            pltpu.VMEM((2, TEAM, WIDE, FOLD * RANK), BF16),
            pltpu.VMEM((2, TEAM, FOLD * RANK, WIDE), BF16),
            pltpu.VMEM(own_rows + (WIDE,), BF16),
            pltpu.VMEM((2, CHUNKS, 2, TILE, RANK), F32),
            pltpu.VMEM(own_rows + (RANK,), BF16),
            pltpu.VMEM(own_rows + (WIDE,), BF16),
            pltpu.VMEM(own_rows + (RANK,), BF16),
            pltpu.VMEM(slot_rows + (WIDE,), BF16),
            pltpu.VMEM((2, TEAM, SHARE, 2, TILE, RANK), F32),
            pltpu.VMEM(slot_rows + (WIDE,), BF16),
            pltpu.VMEM(slot_rows + (RANK,), BF16),
            pltpu.VMEM((2, SHARE, TILE, WIDE), BF16),
            pltpu.VMEM((N_SECTION, 2 * TILE, 2 * RANK), BF16),
            pltpu.VMEM((FOLD, TILE, RANK), BF16),
            pltpu.VMEM((2, N_X, RANK, SHARD), F32),
            pltpu.VMEM(part, BF16),
            pltpu.VMEM(part, BF16),
            pltpu.VMEM((2, 2, 3, RANK, SHARD), BF16),
            pltpu.VMEM((2, 2, 3, RANK, SHARD), BF16),
            pltpu.VMEM((8, 128), F32),
            pltpu.VMEM((N_SECTION, 8, 128), F32),
            pltpu.VMEM((8, 128), F32),
            pltpu.VMEM((N_DP, 8, 128), F32),
            pltpu.VMEM((8, 128), F32),
            dma((2, 2, TEAM)), dma((2, 2, TEAM)),
            dma((2, TEAM, 14)), dma((2, TEAM, 14)),
            dma((2, TEAM)), dma((2, TEAM)),
            dma((2, TEAM)), dma((2, TEAM)),
            dma((2, TEAM, 2)), dma((2, TEAM, 2)),
            dma((2, TEAM, 2)), dma((2, TEAM, 2)),
            dma((2, SHARE)), dma((2, SHARE)),
            dma((TEAM,)), dma((N_SECTION,)),
            dma((2, 2)), dma((2, 2)),
            dma((2, 2, 3)), dma((2, 2, 3)),
            dma, dma((N_SECTION,)),
            dma((N_DP,)), dma((N_DP,)),
            dma((N_SECTION,)), dma,
        ],
        compiler_params=pltpu.CompilerParams(collective_id=0, has_side_effects=True, vmem_limit_bytes=60 << 20),
    )(stash, cot, a_param, b_param)


def adam_update(param, moment, second, grad, clip_factor):
    scaled = clip_factor * grad
    moment_new = beta_one * moment + (1.0 - beta_one) * scaled
    second_new = beta_two * second + (1.0 - beta_two) * scaled * scaled
    param_new = param - learning_rate * moment_new / (jnp.sqrt(second_new) + adam_epsilon)
    return (param_new, moment_new, second_new)


def shards(stash, cotangent, a_param, a_moment, a_second, b_param, b_moment, b_second):
    position = lax.axis_index("section")
    flat = cotangent.reshape(MICRO * TILE, D // N_SECTION)
    cot = lax.dynamic_update_slice(
        jnp.zeros((MICRO * TILE, 2 * RANK), BF16), flat, (0, 32 * lax.rem(position, 4))
    )
    grad_a, grad_b, total = chain(stash[:, 0], cot, a_param[:, 0], b_param[:, 0])
    grad_norm = jnp.sqrt(total[0, 0])
    entries = 4 * N_SECTION * D * RANK
    clip_factor = jnp.minimum(1.0, 0.5 * math.sqrt(entries) / grad_norm)
    a_new, a_moment_new, a_second_new = adam_update(a_param, a_moment, a_second, grad_a[:, None], clip_factor)
    b_new, b_moment_new, b_second_new = adam_update(b_param, b_moment, b_second, grad_b[:, None], clip_factor)
    return (a_new, a_moment_new, a_second_new, b_new, b_moment_new, b_second_new, grad_norm)


def solution(mesh):
    return jax.shard_map(
        shards,
        mesh=mesh,
        in_specs=(
            P(None, "section", None, "dp", None),
            P(None, "dp", "section"),
            P(None, "section", "dp", None),
            P(None, "section", "dp", None),
            P(None, "section", "dp", None),
            P(None, "section", None, "dp"),
            P(None, "section", None, "dp"),
            P(None, "section", None, "dp"),
        ),
        out_specs=(
            P(None, "section", "dp", None),
            P(None, "section", "dp", None),
            P(None, "section", "dp", None),
            P(None, "section", None, "dp"),
            P(None, "section", None, "dp"),
            P(None, "section", None, "dp"),
            P(),
        ),
        check_vma=False,
    )
```

time: 360 us -> 328 us (0.911)
  Pallas kernels: 349 us -> 317 us
    pallas_call x1, Pallas kernels: 349 us -> 317 us  [chain(): pl.pallas_call(chain_kernel, name='chain', out_shape=(jax.ShapeDtypeStruc...]
where the time goes in v2:
time: 328 us
  Pallas kernels  317 us (97%)
  other arithmetic  4.57 us (1%)
    pallas_call x1, Pallas kernels, chain(): pl.pallas_call(chain_kernel, name='chain', out_shape=(jax.ShapeDtypeStruc...  317 us

profile of v2, /device:TPU:1, one launch (start us, length us, event | category | flops | bytes accessed | tf_op | source)
XLA Modules:
  0.0 327.9 jit_solution(6081451848771962024)
XLA Ops:
  0.6 0.0 copy-start
  0.6 0.0 copy-start.2
  0.7 0.0 copy-start.3
  0.7 1.3 dynamic_update_slice.3.cot
  2.0 0.0 copy-start.7
  2.0 0.6 copy-done.7
  2.6 317.4 %chain.1 = (f32[2,640,128]{2,1,0:T(8,128)}, f32[2,128,640]{2,1,0:T(8,128)}, f32[8,128]{1,0:T(8,128)}) custom-call(bf16[2,8,16,5120]{3,2,1,0:T(8,128)(2,1)} %bitcast.85, bf16[128,256]{1,0:T(8,128)(2,1)} %copy-done.7, f32[2,640,128]{2,1,0:T(8,128)} %bitcast.87, f32[2,128,640]{2,1,0:T(8,128)} %bitcast.86), custom_call_target="tpu_custom_call" | custom-call | tf_op jit(solution)/shard_map/chain/pallas_call | solution.py:674
  320.0 0.0 copy-start.1
  320.1 0.0 copy-start.4
  320.1 1.3 slice.3
  322.1 0.0 copy-done
  322.1 0.0 copy-done.2
  322.1 0.0 copy-done.3
  322.1 0.0 copy-start.5
  322.1 0.0 copy-start.6
  322.1 2.9 fusion.8
  325.0 0.0 copy-done.1
  325.0 0.0 copy-done.4
  325.0 0.0 copy-done.5
  325.0 0.0 copy-done.6
  325.0 1.7 fusion.9
  (1 shorter events, 0.0 us)
Async XLA Ops:
  0.6 321.5 %copy-start = (f32[2,1,128,640]{3,2,1,0:T(8,128)S(1)}, f32[2,1,128,640]{3,2,1,0:T(8,128)}, u32[]{:S(2)}) copy-start(f32[2,1,128,640]{3,2,1,0:T(8,128)} %param.13) | copy-start | bytes 1966084
  0.6 321.5 %copy-start.2 = (f32[2,1,128,640]{3,2,1,0:T(8,128)S(1)}, f32[2,1,128,640]{3,2,1,0:T(8,128)}, u32[]{:S(2)}) copy-start(f32[2,1,128,640]{3,2,1,0:T(8,128)} %param.15) | copy-start | bytes 1966084
  0.7 321.5 %copy-start.3 = (f32[2,1,128,640]{3,2,1,0:T(8,128)S(1)}, f32[2,1,128,640]{3,2,1,0:T(8,128)}, u32[]{:S(2)}) copy-start(f32[2,1,128,640]{3,2,1,0:T(8,128)} %param.14) | copy-start | bytes 1966084
  2.0 0.6 copy-start.7
  320.0 5.0 %copy-start.1 = (f32[2,1,640,128]{3,2,1,0:T(8,128)S(1)}, f32[2,1,640,128]{3,2,1,0:T(8,128)}, u32[]{:S(2)}) copy-start(f32[2,1,640,128]{3,2,1,0:T(8,128)} %param.10) | copy-start | bytes 1966084
  320.1 5.0 %copy-start.4 = (f32[2,1,640,128]{3,2,1,0:T(8,128)S(1)}, f32[2,1,640,128]{3,2,1,0:T(8,128)}, u32[]{:S(2)}) copy-start(f32[2,1,640,128]{3,2,1,0:T(8,128)} %param.12) | copy-start | bytes 1966084
  322.1 2.9 copy-start.5
  322.1 2.9 copy-start.6

commit v3 on v2

--- a/solution.py
+++ b/solution.py
@@ -35,8 +35,9 @@
 TEAM = 4
 TEAMS = N_SECTION // TEAM
 SHARE = CHUNKS // TEAM
-HALF = SHARE // 2
-INPUTS, GATES, OPEN, LATE = 1, 2, 3, 7
+PARTS = 4
+PART = SHARE // PARTS
+WEIGHTS, INPUTS, GATES, OPEN, LATE = 0, 1, 2, 3, 7
 BACK = 6
 EARLY = 3
 LAG = 5
@@ -181,7 +182,6 @@
         repeat(0, MICRO, micro)
 
     own_weights(1)
-    own_weights(0)
     for q in range(FOLD):
         mask[q] = jnp.where(group == q, 1.0, 0.0).astype(BF16)
 
@@ -226,26 +226,26 @@
 
     def back_d(u, j, h):
         i = mate(j)
-        src = d_slot.at[u, i, pl.ds(h * HALF, HALF)]
-        dst = d_in.at[u, pl.ds(mine + h * HALF, HALF)]
+        src = d_slot.at[u, i, pl.ds(h * PART, PART)]
+        dst = d_in.at[u, pl.ds(mine + h * PART, PART)]
         return copy(src, dst, rd_s.at[u, i, h], rd_r.at[u, own, h], (base + i, d))
 
     def back_d_in(u, j, h):
         i = mate(j)
-        src = d_slot.at[u, i, pl.ds(h * HALF, HALF)]
-        dst = d_in.at[u, pl.ds(slot_of(i) * SHARE + h * HALF, HALF)]
+        src = d_slot.at[u, i, pl.ds(h * PART, PART)]
+        dst = d_in.at[u, pl.ds(slot_of(i) * SHARE + h * PART, PART)]
         return copy(src, dst, rd_s.at[u, i, h], rd_r.at[u, i, h], (base + i, d))
 
     def back_p(u, j, h):
         i = mate(j)
-        src = p_slot.at[u, i, pl.ds(h * HALF, HALF)]
-        dst = p_in.at[u, pl.ds(mine + h * HALF, HALF)]
+        src = p_slot.at[u, i, pl.ds(h * PART, PART)]
+        dst = p_in.at[u, pl.ds(mine + h * PART, PART)]
         return copy(src, dst, rp_s.at[u, i, h], rp_r.at[u, own, h], (base + i, d))
 
     def back_p_in(u, j, h):
         i = mate(j)
-        src = p_slot.at[u, i, pl.ds(h * HALF, HALF)]
-        dst = p_in.at[u, pl.ds(slot_of(i) * SHARE + h * HALF, HALF)]
+        src = p_slot.at[u, i, pl.ds(h * PART, PART)]
+        dst = p_in.at[u, pl.ds(slot_of(i) * SHARE + h * PART, PART)]
         return copy(src, dst, rp_s.at[u, i, h], rp_r.at[u, i, h], (base + i, d))
 
     for kind in (0, 1):
@@ -372,17 +372,22 @@
 
         repeat(0, SHARE, keep_own)
 
-    def take(u):
+    def take_x(u):
         for j in range(1, TEAM):
             share_x_in(u, j).wait_recv()
+
+    def take_gates(u):
+        for j in range(1, TEAM):
             share_gates_in(u, j).wait_recv()
 
     gather_open(1, own)
+    own_weights(0)
     fold_stash(1)
+    give_x(1)
     gather_close(1, own)
     give_gates(1)
     repeat(1, TEAM, lambda j: gather_next(1, j))
-    give_x(1)
+    fold_stash(0)
 
     @pl.when(first)
     def _():
@@ -414,16 +419,20 @@
 
             refold(lambda q, at: tile(q, at, m), put)
 
+    def lower_weights():
+        for kind in (0, 1):
+            for j in range(1, TEAM):
+                team_weights(0, j, kind).start()
+
+    def lower_inputs():
+        give_x(0)
+
+    take_x(1)
+    pl.when(team >= WEIGHTS)(lower_weights)
+    pl.when(team >= INPUTS)(lower_inputs)
     repeat(1, TEAM, lambda j: gather_close(1, mate(j)))
-    for kind in (0, 1):
-        for j in range(1, TEAM):
-            team_weights(0, j, kind).start()
     gather_open(0, own)
-    take(1)
-
-    def lower_inputs():
-        fold_stash(0)
-        give_x(0)
+    take_gates(1)
 
     def lower_gates():
         gather_close(0, own)
@@ -434,15 +443,13 @@
 
     def lower_close():
         repeat(1, TEAM, lambda j: gather_close(0, mate(j)))
-
-    pl.when(team >= INPUTS)(lower_inputs)
+        take_x(0)
+        take_gates(0)
+
     pl.when(team >= GATES)(lower_gates)
     pl.when(team >= OPEN)(lower_open)
 
-    @pl.when(team >= LATE)
-    def _():
-        lower_close()
-        take(0)
+    pl.when(team >= LATE)(lower_close)
 
     def chain_copy(u, k, dev):
         place = d_slot.at[1, 0, k] if u == 1 else d_slot.at[0, TEAM - 1, k]
@@ -504,19 +511,18 @@
             d_out[0, k] = out
             chain_copy(0, k, up).start()
 
-        @pl.when(first & (k == HALF - 1))
+        @pl.when(first & (k % PART == PART - 1) & (k < SHARE - 1))
         def _():
-            give_back(0, 0)
-
-    def partial(u, kind, e):
-        q = e // PER_PART
-        col = pl.multiple_of((e % PER_PART) * SHARD, SHARD)
+            give_back(0, k // PART)
+
+    def partial(u, kind, h):
         rows = CHUNKS * TILE
         small = hid[u] if kind == 0 else p_in[u]
         right_side = d_in if kind == 0 else x_fold
-        lhs = (small * mask[q][None]).reshape(rows, RANK)
+        lhs = jnp.concatenate([small * mask[q][None] for q in range(FOLD)], axis=2).reshape(rows, FOLD * RANK)
+        col = pl.multiple_of(h * SHARD, SHARD)
         rhs = right_side[u, :, :, pl.ds(col, SHARD)].reshape(rows, SHARD)
-        return lax.dot_general(lhs, rhs, TN, preferred_element_type=F32)
+        return lax.dot_general(lhs, rhs, TN, preferred_element_type=F32).reshape(N_X, RANK, SHARD)
 
     def pair_copy(u, kind):
         return copy(pair_out.at[u, kind], pair_in.at[u, kind], pair_s.at[u, kind], pair_r.at[u, kind], sib)
@@ -531,20 +537,14 @@
 
         repeat(0, SHARE, keep_own)
         for j in range(1, TEAM):
-            for h in (0, 1):
+            for h in range(PARTS):
                 back_d_in(u, j, h).wait_recv()
                 back_p_in(u, j, h).wait_recv()
         for kind in (0, 1):
-            def theirs(i):
-                pair_out[u, kind, i] = partial(u, kind, 2 * i + 1 - c).astype(BF16)
-
-            repeat(0, N_X, theirs)
+            pair_out[u, kind] = partial(u, kind, 1 - c).astype(BF16)
             pair_copy(u, kind).start()
         for kind in (0, 1):
-            def ours(i):
-                keep[kind, i] = partial(u, kind, 2 * i + c)
-
-            repeat(0, N_X, ours)
+            keep[kind] = partial(u, kind, c)
         ways = ((dev_right, right, dev_left, left), (dev_left, left, dev_right, right))
         for kind in (0, 1):
             ahead, ahead_x, behind, behind_x = ways[kind]
@@ -586,20 +586,19 @@
     repeat(0, SHARE, tick)
 
     def back_upper():
-        for h in (0, 1):
-            give_back(1, h)
-
+        repeat(0, PARTS, lambda h: give_back(1, h))
+
+    pl.when(team < WEIGHTS)(lower_weights)
     pl.when(team < INPUTS)(lower_inputs)
     pl.when(team < GATES)(lower_gates)
     pl.when(team < OPEN)(lower_open)
     pl.when(team < LATE)(lower_close)
     pl.when(team < BACK)(back_upper)
     pl.when(team < EARLY)(lambda: gradients(1))
-    pl.when(team < LATE)(lambda: take(0))
     repeat(SHARE - lag, SHARE, lower)
     pl.when(team >= BACK)(back_upper)
-    pl.when(team > 0)(lambda: give_back(0, 0))
-    give_back(0, 1)
+    pl.when(team > 0)(lambda: repeat(0, PARTS - 1, lambda h: give_back(0, h)))
+    give_back(0, PARTS - 1)
     pl.when(team >= EARLY)(lambda: gradients(1))
     gradients(0)
 
@@ -650,7 +649,7 @@
                 team_weights(u, j, kind).wait_send()
             share_x(u, j).wait_send()
             share_gates(u, j).wait_send()
-            for h in (0, 1):
+            for h in range(PARTS):
                 back_d(u, j, h).wait_send()
                 back_p(u, j, h).wait_send()
 
@@ -710,8 +709,8 @@
             dma((2, TEAM, 14)), dma((2, TEAM, 14)),
             dma((2, TEAM)), dma((2, TEAM)),
             dma((2, TEAM)), dma((2, TEAM)),
-            dma((2, TEAM, 2)), dma((2, TEAM, 2)),
-            dma((2, TEAM, 2)), dma((2, TEAM, 2)),
+            dma((2, TEAM, PARTS)), dma((2, TEAM, PARTS)),
+            dma((2, TEAM, PARTS)), dma((2, TEAM, PARTS)),
             dma((2, SHARE)), dma((2, SHARE)),
             dma((TEAM,)), dma((N_SECTION,)),
             dma((2, 2)), dma((2, 2)),

time: 328 us -> 320 us (0.976)
  Pallas kernels: 317 us -> 309 us
    pallas_call x1, Pallas kernels: 317 us -> 309 us  [chain(): pl.pallas_call(chain_kernel, name='chain', out_shape=(jax.ShapeDtypeStruc...]
where the time goes in v3:
time: 320 us; the launch traced here: 319 us
  Pallas kernels  309 us (97%)
  other arithmetic  4.57 us (1%)
  local copies, waits for them, and re-layouts  3.28 us (1%)
    pallas_call x1, Pallas kernels, chain(): pl.pallas_call(chain_kernel, name='chain', out_shape=(jax.ShapeDtypeStruc...  309 us

profile of v3, /device:TPU:1, one launch (start us, length us, event | category | flops | bytes accessed | tf_op | source)
XLA Modules:
  0.0 319.4 jit_solution(9984093867970220981)
XLA Ops:
  0.6 0.0 copy-start
  0.6 0.0 copy-start.2
  0.7 0.0 copy-start.3
  0.7 1.3 dynamic_update_slice.3.cot
  2.0 0.0 copy-start.7
  2.0 0.6 copy-done.7
  2.6 308.9 %chain.1 = (f32[2,640,128]{2,1,0:T(8,128)}, f32[2,128,640]{2,1,0:T(8,128)}, f32[8,128]{1,0:T(8,128)}) custom-call(bf16[2,8,16,5120]{3,2,1,0:T(8,128)(2,1)} %bitcast.85, bf16[128,256]{1,0:T(8,128)(2,1)} %copy-done.7, f32[2,640,128]{2,1,0:T(8,128)} %bitcast.87, f32[2,128,640]{2,1,0:T(8,128)} %bitcast.86), custom_call_target="tpu_custom_call" | custom-call | tf_op jit(solution)/shard_map/chain/pallas_call | solution.py:673
  311.6 0.0 copy-start.1
  311.6 0.0 copy-start.4
  311.6 1.3 slice.3
  313.6 0.0 copy-done
  313.6 0.0 copy-done.2
  313.6 0.0 copy-done.3
  313.6 0.0 copy-start.5
  313.6 0.0 copy-start.6
  313.7 2.9 fusion.8
  316.5 0.0 copy-done.1
  316.5 0.0 copy-done.4
  316.5 0.0 copy-done.5
  316.5 0.0 copy-done.6
  316.6 1.7 fusion.9
  (1 shorter events, 0.0 us)
Async XLA Ops:
  0.6 313.0 %copy-start = (f32[2,1,128,640]{3,2,1,0:T(8,128)S(1)}, f32[2,1,128,640]{3,2,1,0:T(8,128)}, u32[]{:S(2)}) copy-start(f32[2,1,128,640]{3,2,1,0:T(8,128)} %param.13) | copy-start | bytes 1966084
  0.6 313.0 %copy-start.2 = (f32[2,1,128,640]{3,2,1,0:T(8,128)S(1)}, f32[2,1,128,640]{3,2,1,0:T(8,128)}, u32[]{:S(2)}) copy-start(f32[2,1,128,640]{3,2,1,0:T(8,128)} %param.15) | copy-start | bytes 1966084
  0.7 313.0 %copy-start.3 = (f32[2,1,128,640]{3,2,1,0:T(8,128)S(1)}, f32[2,1,128,640]{3,2,1,0:T(8,128)}, u32[]{:S(2)}) copy-start(f32[2,1,128,640]{3,2,1,0:T(8,128)} %param.14) | copy-start | bytes 1966084
  2.0 0.6 copy-start.7
  311.6 5.0 %copy-start.1 = (f32[2,1,640,128]{3,2,1,0:T(8,128)S(1)}, f32[2,1,640,128]{3,2,1,0:T(8,128)}, u32[]{:S(2)}) copy-start(f32[2,1,640,128]{3,2,1,0:T(8,128)} %param.10) | copy-start | bytes 1966084
  311.6 5.0 %copy-start.4 = (f32[2,1,640,128]{3,2,1,0:T(8,128)S(1)}, f32[2,1,640,128]{3,2,1,0:T(8,128)}, u32[]{:S(2)}) copy-start(f32[2,1,640,128]{3,2,1,0:T(8,128)} %param.12) | copy-start | bytes 1966084
  313.6 2.9 copy-start.5
  313.6 2.9 copy-start.6

commit v4 on v3

--- a/solution.py
+++ b/solution.py
@@ -248,10 +248,6 @@
         dst = p_in.at[u, pl.ds(slot_of(i) * SHARE + h * PART, PART)]
         return copy(src, dst, rp_s.at[u, i, h], rp_r.at[u, i, h], (base + i, d))
 
-    for kind in (0, 1):
-        for j in range(1, TEAM):
-            team_weights(1, j, kind).start()
-
     def cot_copy(r):
         src = cot.at[pl.ds(pl.multiple_of(r * 2 * TILE, 2 * TILE), 2 * TILE)]
         return copy(src, window.at[s], cot_s.at[r], cot_r.at[s], (r, d))
@@ -265,6 +261,11 @@
         repeat(0, TEAM, one)
 
     to_first(lambda r: cot_copy(r).start())
+
+    for kind in (0, 1):
+        for j in range(1, TEAM):
+            team_weights(1, j, kind).start()
+
 
     def gather_copy(u, i, at, xs, cs, kind, dev):
         ref = piece(u, i, 2 * xs + cs, kind)
@@ -602,12 +603,20 @@
     pl.when(team >= EARLY)(lambda: gradients(1))
     gradients(0)
 
+    def finish(squares):
+        norm = jnp.sqrt(squares)
+        clip = jnp.minimum(1.0, (0.5 * math.sqrt(4 * N_SECTION * D * RANK)) / norm)[:1, :]
+        total[0, 0] = norm[0, 0]
+        for u in (0, 1):
+            grad_a[u] = grad_a[u] * clip
+            grad_b[u] = grad_b[u] * clip[:, :1]
+
     @pl.when(s > 0)
     def _():
         up_copy = copy(norm_out, norm_in.at[s], nrm_s, nrm_r.at[s], home)
         up_copy.start()
         copy(lane_out, tot_in, lan_s.at[0], tot_r, home).wait_recv()
-        total[...] = tot_in[...]
+        finish(tot_in[...])
         up_copy.wait_send()
 
     @pl.when(s == 0)
@@ -625,9 +634,9 @@
             share(i).wait_recv()
         lane_in[0] = lane_out[...]
         value = jnp.sum(lane_in[...], axis=0)
-        total[...] = value
         norm_out[...] = value
         repeat(1, N_SECTION, lambda i: copy(norm_out, tot_in, tot_s.at[i], tot_r, (i, d)).start())
+        finish(value)
         repeat(1, N_SECTION, lambda i: copy(norm_out, tot_in, tot_s.at[i], tot_r, (i, d)).wait_send())
         for i in range(1, N_DP):
             share(i).wait_send()
@@ -676,10 +685,10 @@
         out_shape=(
             jax.ShapeDtypeStruct((2, SHARD, RANK), F32),
             jax.ShapeDtypeStruct((2, RANK, SHARD), F32),
-            jax.ShapeDtypeStruct((8, 128), F32),
+            jax.ShapeDtypeStruct((1, 1), F32),
         ),
         in_specs=[vmem] * 4,
-        out_specs=(vmem,) * 3,
+        out_specs=(vmem, vmem, pl.BlockSpec(memory_space=pltpu.SMEM)),
         scratch_shapes=[
             pltpu.VMEM((2, TEAM, WIDE, FOLD * RANK), BF16),
             pltpu.VMEM((2, TEAM, FOLD * RANK, WIDE), BF16),
@@ -723,8 +732,7 @@
     )(stash, cot, a_param, b_param)
 
 
-def adam_update(param, moment, second, grad, clip_factor):
-    scaled = clip_factor * grad
+def adam_update(param, moment, second, scaled):
     moment_new = beta_one * moment + (1.0 - beta_one) * scaled
     second_new = beta_two * second + (1.0 - beta_two) * scaled * scaled
     param_new = param - learning_rate * moment_new / (jnp.sqrt(second_new) + adam_epsilon)
@@ -738,11 +746,9 @@
         jnp.zeros((MICRO * TILE, 2 * RANK), BF16), flat, (0, 32 * lax.rem(position, 4))
     )
     grad_a, grad_b, total = chain(stash[:, 0], cot, a_param[:, 0], b_param[:, 0])
-    grad_norm = jnp.sqrt(total[0, 0])
-    entries = 4 * N_SECTION * D * RANK
-    clip_factor = jnp.minimum(1.0, 0.5 * math.sqrt(entries) / grad_norm)
-    a_new, a_moment_new, a_second_new = adam_update(a_param, a_moment, a_second, grad_a[:, None], clip_factor)
-    b_new, b_moment_new, b_second_new = adam_update(b_param, b_moment, b_second, grad_b[:, None], clip_factor)
+    grad_norm = total.reshape(())
+    a_new, a_moment_new, a_second_new = adam_update(a_param, a_moment, a_second, grad_a[:, None])
+    b_new, b_moment_new, b_second_new = adam_update(b_param, b_moment, b_second, grad_b[:, None])
     return (a_new, a_moment_new, a_second_new, b_new, b_moment_new, b_second_new, grad_norm)
 
 

time: 320 us -> 320 us (level)
  no operation moved by 1% of the time
where the time goes in v4:
time: 320 us; the launch traced here: 319 us
  Pallas kernels  310 us (97%)
  other arithmetic  4.57 us (1%)
    pallas_call x1, Pallas kernels, chain(): pl.pallas_call(chain_kernel, name='chain', out_shape=(jax.ShapeDtypeStruc...  310 us

profile of v4, /device:TPU:1, one launch (start us, length us, event | category | flops | bytes accessed | tf_op | source)
XLA Modules:
  0.0 319.4 jit_solution(7619752958096427250)
XLA Ops:
  0.6 0.0 copy-start
  0.6 0.0 copy-start.2
  0.7 0.0 copy-start.3
  0.7 1.3 dynamic_update_slice.3.cot
  2.0 0.0 copy-start.7
  2.0 0.6 copy-done.7
  2.6 310.3 %chain.1 = (f32[2,640,128]{2,1,0:T(8,128)}, f32[2,128,640]{2,1,0:T(8,128)}, f32[1,1]{1,0:T(1,128)}) custom-call(bf16[2,8,16,5120]{3,2,1,0:T(8,128)(2,1)} %bitcast.85, bf16[128,256]{1,0:T(8,128)(2,1)} %copy-done.7, f32[2,640,128]{2,1,0:T(8,128)} %bitcast.86, f32[2,128,640]{2,1,0:T(8,128)} %bitcast.87), custom_call_target="tpu_custom_call" | custom-call | tf_op jit(solution)/shard_map/chain/pallas_call | solution.py:682
  313.0 0.0 copy-start.1
  313.0 0.0 copy-start.4
  313.0 0.0 copy-start.5
  313.0 0.0 copy-start.6
  313.0 0.0 copy-done
  313.0 0.0 copy-done.2
  313.0 0.0 copy-done.3
  313.0 2.9 fusion.9
  315.9 0.0 copy-done.1
  315.9 0.0 copy-done.4
  315.9 0.0 copy-done.5
  316.0 0.0 copy-done.6
  316.0 1.7 fusion.8
  (1 shorter events, 0.0 us)
Async XLA Ops:
  0.6 312.4 %copy-start = (f32[2,1,640,128]{3,2,1,0:T(8,128)S(1)}, f32[2,1,640,128]{3,2,1,0:T(8,128)}, u32[]{:S(2)}) copy-start(f32[2,1,640,128]{3,2,1,0:T(8,128)} %param.10) | copy-start | bytes 1966084
  0.6 312.4 %copy-start.2 = (f32[2,1,640,128]{3,2,1,0:T(8,128)S(1)}, f32[2,1,640,128]{3,2,1,0:T(8,128)}, u32[]{:S(2)}) copy-start(f32[2,1,640,128]{3,2,1,0:T(8,128)} %param.12) | copy-start | bytes 1966084
  0.7 312.4 %copy-start.3 = (f32[2,1,640,128]{3,2,1,0:T(8,128)S(1)}, f32[2,1,640,128]{3,2,1,0:T(8,128)}, u32[]{:S(2)}) copy-start(f32[2,1,640,128]{3,2,1,0:T(8,128)} %param.11) | copy-start | bytes 1966084
  2.0 0.6 copy-start.7
  313.0 3.0 copy-start.1
  313.0 3.0 copy-start.4
  313.0 3.0 copy-start.5
  313.0 3.0 copy-start.6
